TPU v7x, 256 devices: a whole 4x4x8 slice. The times are simulated.
256 devices in a mesh: dp: 16 (over x, y), mp: 16 (over z, core).
Axes of the slice: x: 4, y: 4, z: 8, core: 2. Of those that a mesh axis runs over, the one named last changes fastest.
Arguments:
- hidden_in: bfloat16 [2048, 8192], P('dp', 'mp'), may hold values from -256 to 256
- out_grad: bfloat16 [2048, 8192], P('dp', 'mp'), may hold values from -1.796875 to 1.796875
- neighbours: bfloat16 [512, 128, 1536], P('dp', 'mp'), may hold values from -6 to 6
- counts: int32 [32], P('dp'), may hold values from 2 to 10, as said below
- slot_owner: int32 [512], P('dp'), may hold values from -1 to 319, as said below
- w_query: bfloat16 [8192, 4096], P(None, 'mp'), may hold values from -0.0625 to 0.0625
- w_key: bfloat16 [1536, 4096], P(None, 'mp'), may hold values from -0.15625 to 0.15625
- w_value: bfloat16 [1536, 4096], P(None, 'mp'), may hold values from -0.15625 to 0.15625
- w_out: bfloat16 [4096, 8192], P('mp'), may hold values from -0.59765625 to 0.59765625
Outputs:
- layer_out: bfloat16 [2048, 8192], P('dp', 'mp')
- neighbour_grad: bfloat16 [512, 128, 1536], P('dp', 'mp')
Inputs may be any that keep to these rules, and one draw needn't show every extreme that they name: `counts`: every draw has one decoder group (spans g * 2 to g * 2 + 1) whose spans all have 10 neighbours. `slot_owner`: entry i is the span slot c * 10 + j that encoder slot i fills, or -1 for an empty encoder slot. Each slot with j < counts[c] is named exactly once, no other slot is named. The 32 entries of one index of dp name at most 2 slots of the spans of one decoder group (spans g * 2 to g * 2 + 1), and in every draw some index of dp names exactly 2 for some group.
All inputs are finite; a program needn't handle non-finite values.
Results may differ from a plain program's by a relative error of at most 0.024.
Values may be sent and summed in bfloat16 or wider, within the bound.
No kernel may reach another device: no remote copies, remote signals or barrier semaphores. Data moves between devices by JAX's collectives and lax.ppermute only.
A program may use at most 128 MiB of HBM per device.

v0:
```python
import functools
import math

import jax
import jax.numpy as jnp
from jax import lax
from jax.experimental import pallas as pl
from jax.experimental.pallas import tpu as pltpu
from jax.sharding import PartitionSpec as P

DH = 128
MAXN = 10
BF = jnp.bfloat16
F32 = jnp.float32
LAST = (((1,), (1,)), ((), ()))
FIRST = (((0,), (0,)), ((), ()))


def dot(a, b):
    return jnp.dot(a, b, preferred_element_type=F32)


def dot_t(a, b):
    return lax.dot_general(a, b, LAST, preferred_element_type=F32)


def chip_shift(value, step):
    devices = lax.axis_size("mp")
    chips = devices // 2
    pairs = [
        (2 * z + c, 2 * ((z + step) % chips) + c) for z in range(chips) for c in range(2)
    ]
    return lax.ppermute(value, "mp", pairs)


def core_swap(value):
    return lax.ppermute(value, "mp", [(i, i ^ 1) for i in range(lax.axis_size("mp"))])


def after(values, first):
    return lax.optimization_barrier((values, first))[0]


def ring_step(ups, downs):
    return [chip_shift(u, 1) for u in ups], [chip_shift(d, -1) for d in downs]


def to_bf16(values):
    return [v.astype(BF) for v in values]


VMEM_LIMIT = 40 * 2**20


def in_vmem(count):
    return [pl.BlockSpec(memory_space=pltpu.VMEM)] * count


def out_kernel(core, attended, w_out, mine, other):
    width = w_out.shape[1] // 2
    parts = [dot(attended[...], w_out[:, i * width : (i + 1) * width]) for i in range(2)]
    first = core[0] == 0
    mine[0] = jnp.where(first, parts[0], parts[1])
    other[0] = jnp.where(first, parts[1], parts[0])


def project_out(core, attended, w_out, chips):
    tokens, features = attended.shape
    width = w_out.shape[1] // (2 * chips)
    out = jax.ShapeDtypeStruct((chips, tokens, width), F32)
    return pl.pallas_call(
        out_kernel,
        out_shape=(out, out),
        grid_spec=pltpu.PrefetchScalarGridSpec(
            num_scalar_prefetch=1,
            grid=(chips,),
            in_specs=[
                pl.BlockSpec((tokens, features), lambda i, p: (0, 0)),
                pl.BlockSpec((features, 2 * width), lambda i, p: (0, i)),
            ],
            out_specs=[
                pl.BlockSpec((1, tokens, width), lambda i, p: (i, 0, 0)),
                pl.BlockSpec((1, tokens, width), lambda i, p: (i, 0, 0)),
            ],
        ),
        compiler_params=pltpu.CompilerParams(vmem_limit_bytes=VMEM_LIMIT),
        cost_estimate=pl.CostEstimate(
            flops=4 * tokens * features * width * chips,
            bytes_accessed=4 * chips * width * (features + 4 * tokens),
            transcendentals=0,
        ),
    )(core, attended, w_out)


def lines_kernel(own, partner, key_own, value_own, key_partner, value_partner, lines):
    length, width = own.shape
    heads = width // (2 * DH)
    for kind, weights in enumerate(((key_own, key_partner), (value_own, value_partner))):
        for i, (pair, weight) in enumerate(zip((own, partner), weights)):
            for h in range(heads):
                part = slice((kind * heads + h) * DH, (kind * heads + h + 1) * DH)
                first = ((kind * 2 + i) * heads + h) * length
                made = dot_t(pair[:, part], weight[:, h * DH : (h + 1) * DH])
                high = made.astype(BF)
                lines[first : first + length] = high
                if kind == 0:
                    first += 4 * heads * length
                    lines[first : first + length] = (made - high.astype(F32)).astype(BF)


def make_lines(own, partner, weights):
    length, width = own.shape
    enc = weights[0].shape[0]
    rows = 3 * length * width // DH
    return pl.pallas_call(
        lines_kernel,
        out_shape=jax.ShapeDtypeStruct((rows, enc), BF),
        in_specs=in_vmem(6),
        out_specs=in_vmem(1)[0],
        compiler_params=pltpu.CompilerParams(vmem_limit_bytes=VMEM_LIMIT),
        cost_estimate=pl.CostEstimate(
            flops=2 * rows * DH * enc, bytes_accessed=4 * rows * enc, transcendentals=0
        ),
    )(own, partner, *weights)


def gather(refs, keys):
    first = 0
    for ref in refs:
        keys[first : first + ref.shape[0]] = ref[...]
        first += ref.shape[0]


def products(lines, keys, out):
    step = 2 * DH

    @pl.loop(0, lines.shape[0] // step)
    def _(i):
        rows = pl.ds(pl.multiple_of(i * step, step), step)
        out[rows] = dot_t(lines[rows], keys[...])


def products_kernel(lines, *refs):
    out, keys = refs[-2:]
    gather(refs[:-2], keys)
    products(lines, keys, out)


def make_products(lines, chunks):
    rows, enc = lines.shape
    count = sum(c.shape[0] for c in chunks)
    return pl.pallas_call(
        products_kernel,
        out_shape=jax.ShapeDtypeStruct((rows, count), F32),
        in_specs=in_vmem(1 + len(chunks)),
        out_specs=in_vmem(1)[0],
        scratch_shapes=[pltpu.VMEM((count, enc), BF)],
        compiler_params=pltpu.CompilerParams(vmem_limit_bytes=VMEM_LIMIT),
        cost_estimate=pl.CostEstimate(
            flops=2 * rows * count * enc,
            bytes_accessed=2 * enc * (rows + count) + 4 * rows * count,
            transcendentals=0,
        ),
    )(lines, *chunks)


def softmax_kernel(scale, per_slot, period, late, count, lines, early, *refs):
    keys, last, *columns_refs = refs[-4:]
    weights_out, grads_out = refs[late : late + 2], refs[late + 2 : -4]
    gather(refs[:late], keys)
    products(lines, keys, last)
    both = [early[...], last[...]]
    middle = lines.shape[0] // 3
    scores = []
    for product in both:
        columns = lax.broadcasted_iota(jnp.int32, (middle, product.shape[1]), 1)
        live = (columns % period) // per_slot < count[0]
        score = (product[:middle] + product[2 * middle :]) * scale
        scores.append(jnp.where(live, score, -jnp.inf))
    peak = functools.reduce(
        jnp.maximum, [jnp.max(part, axis=-1, keepdims=True) for part in scores]
    )
    exponents = [jnp.exp(part - peak) for part in scores]
    total = sum(jnp.sum(part, axis=-1, keepdims=True) for part in exponents)
    weights = [part / total for part in exponents]
    inner = sum(
        jnp.sum(w * p[middle : 2 * middle], axis=-1, keepdims=True)
        for w, p in zip(weights, both)
    )
    for weight, product, out, columns in zip(weights, both, weights_out, columns_refs):
        score = weight * (product[middle : 2 * middle] - inner) * scale
        rounded = weight.astype(BF)
        out[...] = rounded
        columns[:middle] = score.astype(BF)
        columns[middle:] = rounded
    step = 4 * DH

    @pl.loop(0, lines.shape[1] // step)
    def _(i):
        part = pl.ds(pl.multiple_of(i * step, step), step)
        right = lines[: 2 * middle, part]
        place = 0
        for columns in columns_refs:
            made = lax.dot_general(columns[...], right, FIRST, preferred_element_type=F32)
            first = 0
            while first < made.shape[0]:
                out = grads_out[place]
                out[:, part] = made[first : first + out.shape[0]].astype(out.dtype)
                first += out.shape[0]
                place += 1


def make_softmax(count, lines, early, chunks, per_slot, shapes, scale):
    rows, enc = lines.shape
    late = sum(c.shape[0] for c in chunks)
    keys = early.shape[1] + late
    period = shapes[0][0]
    return pl.pallas_call(
        functools.partial(softmax_kernel, scale, per_slot, period, len(chunks)),
        out_shape=[
            jax.ShapeDtypeStruct((rows // 3, early.shape[1]), BF),
            jax.ShapeDtypeStruct((rows // 3, late), BF),
        ]
        + [jax.ShapeDtypeStruct((n, enc), kind) for n, kind in shapes],
        in_specs=[pl.BlockSpec(memory_space=pltpu.SMEM)] + in_vmem(2 + len(chunks)),
        out_specs=in_vmem(2 + len(shapes)),
        scratch_shapes=[
            pltpu.VMEM((late, enc), BF),
            pltpu.VMEM((rows, late), F32),
            pltpu.VMEM((rows // 3 * 2, early.shape[1]), BF),
            pltpu.VMEM((rows // 3 * 2, late), BF),
        ],
        compiler_params=pltpu.CompilerParams(vmem_limit_bytes=VMEM_LIMIT),
        cost_estimate=pl.CostEstimate(
            flops=2 * rows * (late + keys) * enc,
            bytes_accessed=2 * enc * (rows + late + 2 * keys) + 4 * rows * keys,
            transcendentals=rows * keys // 2,
        ),
    )(count, lines, early, *chunks)


def attended_kernel(first, second, value_own, value_partner, *refs):
    own, partner, keys, high, low = refs[-5:]
    gather(refs[:-5], keys)
    split, step = first.shape[1], 4 * DH

    @pl.loop(0, keys.shape[1] // step)
    def _(i):
        part = pl.ds(pl.multiple_of(i * step, step), step)
        mixed = dot(first[...], keys[:split, part]) + dot(second[...], keys[split:, part])
        rounded = mixed.astype(BF)
        high[:, part] = rounded
        low[:, part] = (mixed - rounded.astype(F32)).astype(BF)

    length, width = own.shape
    for i, (weight, out) in enumerate(((value_own, own), (value_partner, partner))):
        for h in range(width // DH):
            rows = slice((i * (width // DH) + h) * length, (i * (width // DH) + h + 1) * length)
            part = slice(h * DH, (h + 1) * DH)
            made = dot(high[rows], weight[:, part]) + dot(low[rows], weight[:, part])
            out[:, part] = made.astype(BF)


def make_attended(weights, values, early, late, length):
    rows, enc = weights[0].shape[0], values[0].shape[0]
    keys = weights[0].shape[1] + weights[1].shape[1]
    out = jax.ShapeDtypeStruct((length, values[0].shape[1]), BF)
    return pl.pallas_call(
        attended_kernel,
        out_shape=(out, out),
        in_specs=in_vmem(4 + len(early) + len(late)),
        out_specs=in_vmem(2),
        scratch_shapes=[pltpu.VMEM((n, enc), BF) for n in (keys, rows, rows)],
        compiler_params=pltpu.CompilerParams(vmem_limit_bytes=VMEM_LIMIT),
        cost_estimate=pl.CostEstimate(
            flops=2 * rows * keys * enc, bytes_accessed=2 * keys * (rows + enc), transcendentals=0
        ),
    )(*weights, *values, *early, *late)


def pick_kernel(parts, source, rows, *outs):
    count, _, width = outs[0].shape
    for k in range(parts):

        @pl.loop(0, count)
        def _(i, k=k):
            index = source[k * count + i]
            value = rows[jnp.maximum(index, 0), :, :width]
            outs[k][i] = jnp.where(index >= 0, value, jnp.zeros_like(value))


def join_kernel(source, first, second, out):
    split = first.shape[0]

    @pl.loop(0, out.shape[0])
    def _(i):
        low = jnp.minimum(jnp.maximum(source[i], 0), split - 1)
        high = jnp.maximum(source[i] - split, 0)
        out[i] = jnp.where(source[i] < split, first[low], second[high])


def join_pick(first, second, source):
    shape = (source.shape[0],) + first.shape[1:]
    return pl.pallas_call(
        join_kernel,
        out_shape=jax.ShapeDtypeStruct(shape, BF),
        in_specs=[pl.BlockSpec(memory_space=pltpu.SMEM)] + in_vmem(2),
        out_specs=in_vmem(1)[0],
        cost_estimate=pl.CostEstimate(
            flops=0, bytes_accessed=4 * math.prod(shape), transcendentals=0
        ),
    )(source.astype(jnp.int32), first, second)


def pick(rows, source, width=None, parts=1):
    shape = (source.shape[0] // parts, rows.shape[1], width or rows.shape[2])
    return pl.pallas_call(
        functools.partial(pick_kernel, parts),
        out_shape=[jax.ShapeDtypeStruct(shape, BF)] * parts,
        in_specs=[pl.BlockSpec(memory_space=pltpu.SMEM)] + in_vmem(1),
        out_specs=in_vmem(parts),
        cost_estimate=pl.CostEstimate(
            flops=0, bytes_accessed=4 * parts * math.prod(shape), transcendentals=0
        ),
    )(source.astype(jnp.int32), rows)


def pack_kernel(slots_group, owner, rows, hidden, grad, out, position, both, counts):
    both[: hidden.shape[0]] = hidden[...]
    both[hidden.shape[0] :] = grad[...]
    count, height, width = rows.shape
    capacity = count // counts.shape[0]
    out[:, :, width:] = jnp.full((count, height, DH), -1, BF)
    for g in range(counts.shape[0]):
        counts[g] = 0

    @pl.loop(0, count)
    def _(i):
        slot = owner[i]
        position[i] = -1

        @pl.when(slot >= 0)
        def _():
            group = slot // slots_group
            place = group * capacity + counts[group]
            counts[group] += 1
            position[i] = place
            out[place, :, :width] = rows[i]
            tag = (slot - group * slots_group).astype(F32)
            out[place, :, width:] = jnp.full((height, DH), tag).astype(BF)


def pack(rows, hidden, grad, owner, groups, slots_group):
    count, height, width = rows.shape
    return pl.pallas_call(
        functools.partial(pack_kernel, slots_group),
        out_shape=(
            jax.ShapeDtypeStruct((count, height, width + DH), BF),
            jax.ShapeDtypeStruct((count,), jnp.int32),
            jax.ShapeDtypeStruct((2 * hidden.shape[0], hidden.shape[1]), BF),
        ),
        in_specs=[pl.BlockSpec(memory_space=pltpu.SMEM)] + in_vmem(3),
        out_specs=in_vmem(1) + [pl.BlockSpec(memory_space=pltpu.SMEM)] + in_vmem(1),
        scratch_shapes=[pltpu.SMEM((groups,), jnp.int32)],
        cost_estimate=pl.CostEstimate(
            flops=0, bytes_accessed=4 * math.prod(rows.shape), transcendentals=0
        ),
    )(owner, rows, hidden, grad)


def per_device(hidden_in, out_grad, neighbours, counts, slot_owner, w_query, w_key, w_value, w_out):
    groups = lax.axis_size("dp")
    spans = counts.shape[0]
    slots_group = spans * MAXN
    src_slots = slot_owner.shape[0]
    capacity = src_slots // groups
    reach = lax.axis_size("mp") // 4
    rows_dev = neighbours.shape[1]
    enc_width = neighbours.shape[2]
    tokens_dev = hidden_in.shape[0]
    span_len = tokens_dev // spans
    devices = lax.axis_size("mp")
    chips = devices // 2
    core = (lax.axis_index("mp") % 2).astype(jnp.int32)

    slot_order = jnp.arange(src_slots, dtype=jnp.int32)
    send_rows, position, both = pack(
        neighbours, hidden_in, out_grad, slot_owner, groups, slots_group
    )
    both = lax.all_gather(both, "mp", axis=1, tiled=True)
    got = lax.all_to_all(
        send_rows.reshape(groups, capacity, rows_dev, enc_width + DH),
        "dp",
        split_axis=0,
        concat_axis=0,
        tiled=True,
    ).reshape(src_slots, rows_dev, enc_width + DH)
    local_slot = got[:, 0, enc_width].astype(jnp.int32)
    slots = jnp.arange(slots_group, dtype=jnp.int32)
    wanted = (slots + core * MAXN) % slots_group
    matches = local_slot[None, :] == wanted[:, None]
    chosen = jnp.sum(jnp.where(matches, slot_order[None, :] + 1, 0), axis=1) - 1
    returns = jnp.maximum(jnp.where(core == 0, local_slot, (local_slot + MAXN) % slots_group), 0)
    chunk_rows = MAXN * rows_dev
    kept, given = pick(got, chosen, enc_width, spans)
    kept, given = kept.reshape(chunk_rows, enc_width), given.reshape(chunk_rows, enc_width)
    given = core_swap(given)
    w_key_partner, w_value_partner = core_swap(w_key), core_swap(w_value)
    queries = dot(both[:tokens_dev], w_query).astype(BF)
    grad_attended = dot_t(both[tokens_dev:], w_out).astype(BF)
    pair = jnp.concatenate([queries, grad_attended], axis=1)
    ups, downs = [kept, given], [kept, given]
    keys = [kept, given]
    for step in range(1, reach):
        ups, downs = ring_step(ups, downs)
        keys += ups + downs
    tokens = [
        lax.dynamic_slice_in_dim(pair, c * span_len, span_len, 0) for c in (core, 1 - core)
    ]
    lines = make_lines(
        tokens[0], core_swap(tokens[1]), (w_key, w_value, w_key_partner, w_value_partner)
    )
    ups[0], downs[1] = after([ups[0], downs[1]], lines)
    keys += [chip_shift(ups[0], 1), chip_shift(downs[1], -1)]
    first_late = 2 + 4 * (reach - 2)
    early, late = keys[:first_late], keys[first_late:]

    count = lax.dynamic_slice_in_dim(counts, core, 1)
    shapes = [(chunk_rows, BF)] * len(keys)
    outs = make_softmax(
        count,
        lines,
        make_products(lines, early),
        late,
        rows_dev,
        shapes,
        1.0 / math.sqrt(DH),
    )
    weights, grads = outs[:2], outs[2:]
    attended, away = make_attended(weights, (w_value, w_value_partner), early, late, span_len)
    back = core_swap(away)
    attended = jnp.where(
        core == 0,
        jnp.concatenate([attended, back], axis=0),
        jnp.concatenate([back, attended], axis=0),
    )
    mine, other = project_out(core.reshape(1), attended, w_out, chips)
    sums = (mine + core_swap(other)).astype(BF)

    def part(distance, ring):
        return grads[4 * abs(distance) - 2 + (2 if distance > 0 else 0) + ring]

    chains = [
        (0, 1, reach, grads[-2]),
        (1, 1, reach - 1, part(reach - 1, 1)),
        (0, -1, reach - 1, part(1 - reach, 0)),
        (1, -1, reach, grads[-1]),
    ]
    scattered = [grads[0].astype(F32), grads[1].astype(F32)]
    for step in range(reach):
        moved = []
        for ring, way, left, value in chains:
            value = chip_shift(value, way).astype(F32)
            if left > 1:
                value = (value + part(way * (left - 1), ring)).astype(BF)
                moved.append((ring, way, left - 1, value))
            else:
                scattered[ring] = scattered[ring] + value
        chains = moved
    scattered = to_bf16(scattered)
    scattered[1] = core_swap(scattered[1])
    scattered = [part.reshape(MAXN, rows_dev, enc_width) for part in scattered]

    layer_out = lax.psum_scatter(
        sums,
        "mp",
        scatter_dimension=0,
        axis_index_groups=[list(range(c, devices, 2)) for c in range(2)],
    )

    returned = lax.all_to_all(
        join_pick(*scattered, returns).reshape(groups, capacity, rows_dev, enc_width),
        "dp",
        split_axis=0,
        concat_axis=0,
        tiled=True,
    ).reshape(src_slots, rows_dev, enc_width)
    neighbour_grad = pick(returned, position)[0]
    return (layer_out, neighbour_grad)


def solution(mesh):
    return jax.shard_map(
        per_device,
        mesh=mesh,
        in_specs=(
            P("dp", "mp"),
            P("dp", "mp"),
            P("dp", "mp", None),
            P("dp"),
            P("dp"),
            P(None, "mp"),
            P(None, "mp"),
            P(None, "mp"),
            P("mp", None),
        ),
        out_specs=(P("dp", "mp"), P("dp", "mp", None)),
        check_vma=False,
    )
```

profile of v0, /device:TPU:2, one launch (start us, length us, event | category | flops | bytes accessed | tf_op | source)
XLA Modules:
  0.0 192.8 jit_solution(7623370251387234480)
XLA Ops:
  7.2 2.9 %shard_map.104 = (bf16[32,8,1664]{2,1,0:T(8,128)(2,1)}, s32[32]{0:T(128)}, bf16[256,512]{1,0:T(8,128)(2,1)}) custom-call(s32[32]{0:T(128)} %owner.1, bf16[32,8,1536]{2,1,0:T(8,128)(2,1)} %rows.1, bf16[128,512]{1,0:T(8,128)(2,1)} %hidden.1, bf16[128,512]{1,0:T(8,128)(2,1)} %grad.1), custom_call_target="tpu_custom_call" | custom-call | bytes 1572864 | tf_op jit(solution)/shard_map/pallas_call | solution.py:355
  10.2 7.4 %all-to-all-start = ((bf16[16,2,8,1664]{3,2,1,0:T(8,128)(2,1)}), bf16[16,2,8,1664]{3,2,1,0:T(8,128)(2,1)S(1)}, u32[]{:S(2)}, u32[]{:S(2)}) async-start(bf16[16,2,8,1664]{3,2,1,0:T(8,128)(2,1)} %bitcast.21), calls=%async_computation | async-start | bytes 1703936 | tf_op jit(solution)/shard_map/all_to_all | solution.py:391
  17.8 12.5 %all-to-all-done = bf16[16,2,8,1664]{3,2,1,0:T(8,128)(2,1)S(1)} async-done(((bf16[16,2,8,1664]{3,2,1,0:T(8,128)(2,1)}), bf16[16,2,8,1664]{3,2,1,0:T(8,128)(2,1)S(1)}, u32[]{:S(2)}, u32[]{:S(2)}) %all-to-all-start) | async-done | bytes 852000 | tf_op jit(solution)/shard_map/all_to_all | solution.py:391
  30.3 0.7 fusion.13
  31.1 0.6 broadcast_add_fusion.source
  31.7 2.1 %shard_map.106 = (bf16[10,8,1536]{2,1,0:T(8,128)(2,1)}, bf16[10,8,1536]{2,1,0:T(8,128)(2,1)}) custom-call(s32[20]{0:T(128)} %broadcast_add_fusion.source, bf16[32,8,1664]{2,1,0:T(8,128)(2,1)} %bitcast.18), custom_call_target="tpu_custom_call" | custom-call | bytes 983040 | tf_op jit(solution)/shard_map/pallas_call | solution.py:317
  33.9 1.9 collective-permute-start.4
  35.8 5.7 %collective-permute-start.7 = (bf16[80,1536]{1,0:T(8,128)(2,1)S(1)}, bf16[80,1536]{1,0:T(8,128)(2,1)S(1)}, u32[]{:S(2)}, u32[]{:S(2)}) collective-permute-start(bf16[80,1536]{1,0:T(8,128)(2,1)S(1)} %collective-permute-done.3.refs_1_), channel_id=1, source_target_pairs={{0,14},{1,15},{2,0},{3,1},{4,2},{5,3},{6,4},{7,5},{8,6},{9,7},{10,... | collective-permute-start | bytes 737288 | tf_op jit(solution)/shard_map/ppermute | solution.py:33
  41.4 1.0 collective-permute-start.6
  42.4 1.0 collective-permute-start.5
  43.5 8.1 %collective-permute-done.4.refs_2_ = bf16[80,1536]{1,0:T(8,128)(2,1)S(1)} collective-permute-done((bf16[80,1536]{1,0:T(8,128)(2,1)}, bf16[80,1536]{1,0:T(8,128)(2,1)S(1)}, u32[]{:S(2)}, u32[]{:S(2)}) %collective-permute-start.4) | collective-permute-done | bytes 245792 | tf_op jit(solution)/shard_map/ppermute | solution.py:33
  51.6 0.7 collective-permute-done.7.refs_5_
  52.3 3.7 %collective-permute-start.11 = (bf16[80,1536]{1,0:T(8,128)(2,1)S(1)}, bf16[80,1536]{1,0:T(8,128)(2,1)}, u32[]{:S(2)}, u32[]{:S(2)}) collective-permute-start(bf16[80,1536]{1,0:T(8,128)(2,1)S(1)} %collective-permute-done.7.refs_5_), channel_id=1, source_target_pairs={{0,14},{1,15},{2,0},{3,1},{4,2},{5,3},{6,4},{7,5},{8,6},{9,7},{10,... | collective-permute-start | bytes 737288 | tf_op jit(solution)/shard_map/ppermute | solution.py:33
  56.0 6.7 %all-gather.2.cloned.1.call-done = bf16[256,8192]{1,0:T(8,128)(2,1)} async-done(((bf16[256,512]{1,0:T(8,128)(2,1)}), bf16[256,8192]{1,0:T(8,128)(2,1)}) %all-gather.2.cloned.1.call-update) | async-done | bytes 4194320 | tf_op jit(solution)/shard_map/all_gather | solution.py:390
  62.7 3.7 %fusion.4 = bf16[128,256]{1,0:T(8,128)(2,1)S(1)} fusion(bf16[8192,256]{1,0:T(8,128)(2,1)} %param.14, bf16[256,8192]{1,0:T(8,128)(2,1)} %all-gather.2.cloned.1.call-done), kind=kOutput, calls=%fused_computation.5 | convolution fusion | flops 536903680 | bytes 6356992 | tf_op jit(solution)/shard_map/dot_general | solution.py:20
  66.4 1.5 collective-permute-start.10
  67.9 0.6 collective-permute-start.12
  68.5 0.8 collective-permute-start.9
  69.3 2.4 %collective-permute-start.15 = (bf16[80,1536]{1,0:T(8,128)(2,1)}, bf16[80,1536]{1,0:T(8,128)(2,1)}, u32[]{:S(2)}, u32[]{:S(2)}) collective-permute-start(bf16[80,1536]{1,0:T(8,128)(2,1)} %collective-permute-done.11.refs_9_), channel_id=1, source_target_pairs={{0,14},{1,15},{2,0},{3,1},{4,2},{5,3},{6,4},{7,5},{8,6},{9,7},{10,... | collective-permute-start | bytes 737288 | tf_op jit(solution)/shard_map/ppermute | solution.py:33
  71.7 3.1 %fusion.7 = bf16[128,256]{1,0:T(8,128)(2,1)S(1)} fusion(bf16[256,8192]{1,0:T(8,128)(2,1)S(1)} %copy-done, bf16[256,8192]{1,0:T(8,128)(2,1)} %all-gather.2.cloned.1.call-done), kind=kOutput, calls=%fused_computation.6 | convolution fusion | flops 536903680 | bytes 6356992 | tf_op jit(solution)/shard_map/dot_general | solution.py:24
  75.0 0.3 collective-permute-start
  75.4 2.6 %collective-permute-start.14 = (bf16[80,1536]{1,0:T(8,128)(2,1)}, bf16[80,1536]{1,0:T(8,128)(2,1)}, u32[]{:S(2)}, u32[]{:S(2)}) collective-permute-start(bf16[80,1536]{1,0:T(8,128)(2,1)} %collective-permute-done.10.refs_8_), channel_id=1, source_target_pairs={{0,14},{1,15},{2,0},{3,1},{4,2},{5,3},{6,4},{7,5},{8,6},{9,7},{10,... | collective-permute-start | bytes 737288 | tf_op jit(solution)/shard_map/ppermute | solution.py:33
  78.0 4.5 %collective-permute-done.9.refs_7_ = bf16[80,1536]{1,0:T(8,128)(2,1)} collective-permute-done((bf16[80,1536]{1,0:T(8,128)(2,1)S(1)}, bf16[80,1536]{1,0:T(8,128)(2,1)}, u32[]{:S(2)}, u32[]{:S(2)}) %collective-permute-start.9) | collective-permute-done | bytes 245792 | tf_op jit(solution)/shard_map/ppermute | solution.py:33
  82.5 1.1 copy-done.4
  83.6 2.3 %shard_map.105.lines = bf16[768,1536]{1,0:T(8,128)(2,1)S(1)} custom-call(bf16[64,512]{1,0:T(8,128)(2,1)S(1)} %get-tuple-element.61.own, bf16[64,512]{1,0:T(8,128)(2,1)S(1)} %collective-permute-done.partner, bf16[1536,256]{1,0:T(8,128)(2,1)S(1)} %copy-done.22, bf16[1536,256]{1,0:T(8,128)(2,1)S(1)} %copy-done.2, ...), custom_call_target="tpu_custom_call" | custom-call | flops 301989888 | bytes 4718592 | tf_op jit(solution)/shard_map/pallas_call | solution.py:115
  86.0 0.3 collective-permute-start.16
  86.3 3.1 %collective-permute-start.17 = (bf16[80,1536]{1,0:T(8,128)(2,1)}, bf16[80,1536]{1,0:T(8,128)(2,1)}, u32[]{:S(2)}, u32[]{:S(2)}) collective-permute-start(bf16[80,1536]{1,0:T(8,128)(2,1)} %collective-permute-done.15.refs_3_.refs_13_), channel_id=1, source_target_pairs={{0,14},{1,15},{2,0},{3,1},{4,2},{5,3},{6,4},{7,5},{8,6},{9,7},{10,... | collective-permute-start | bytes 737288 | tf_op jit(solution)/shard_map/ppermute | solution.py:33
  89.4 0.6 dynamic_slice.9.count
  90.0 0.9 copy-done.8
  90.9 0.9 copy-done.11
  91.8 0.9 copy-done.14
  92.8 0.9 copy-done.17
  93.7 0.9 copy-done.20
  94.7 4.5 %shard_map.107.early = f32[768,800]{1,0:T(8,128)S(1)} custom-call(bf16[768,1536]{1,0:T(8,128)(2,1)S(1)} %shard_map.105.lines, bf16[80,1536]{1,0:T(8,128)(2,1)S(1)} %bitcast.15, bf16[80,1536]{1,0:T(8,128)(2,1)S(1)} %copy-done.8, bf16[80,1536]{1,0:T(8,128)(2,1)S(1)} %copy-done.11, bf16[80,1536]{1,0:T(8,128)(2,1)S(1)} %copy-done.20, ...), custom_call_target="tpu_custom_call" | custom-call | flops 1887436800 | bytes 7274496 | tf_op jit(solution)/shard_map/pallas_call | solution.py:152
  99.3 7.6 %shard_map.108 = (bf16[256,800]{1,0:T(8,128)(2,1)S(1)}, bf16[256,480]{1,0:T(8,128)(2,1)S(1)}, bf16[80,1536]{1,0:T(8,128)(2,1)S(1)}, bf16[80,1536]{1,0:T(8,128)(2...) custom-call(s32[1]{0:T(128)} %dynamic_slice.9.count, ...), custom_call_target="tpu_custom_call" | custom-call | flops 4152360960 | bytes 15630336 | tf_op jit(solution)/shard_map/pallas_call | solution.py:218
  106.8 0.7 copy-done.23
  107.5 0.7 copy-done.27
  108.3 4.4 %shard_map.109 = (bf16[64,256]{1,0:T(8,128)(2,1)S(1)}, bf16[64,256]{1,0:T(8,128)(2,1)S(1)}) custom-call(bf16[256,800]{1,0:T(8,128)(2,1)S(1)} %get-tuple-element.37.first, bf16[256,480]{1,0:T(8,128)(2,1)S(1)} %get-tuple-element.38.second, bf16[1536,256]{1,0:T(8,128)(2,1)S(1)} %copy-done.2, bf16[1536,256]{1,0:T(8,128)(2,1)S(1)} %copy-done.5, ...), custom_call_target="tpu_custom_call" | custom-call | flops 1006632960 | bytes 4587520 | tf_op jit(solution)/shard_map/pallas_call | solution.py:268
  112.8 0.6 fusion.14.source
  113.4 3.1 %collective-permute-start.30 = (bf16[80,1536]{1,0:T(8,128)(2,1)S(1)}, bf16[80,1536]{1,0:T(8,128)(2,1)S(1)}, u32[]{:S(2)}, u32[]{:S(2)}) collective-permute-start(bf16[80,1536]{1,0:T(8,128)(2,1)S(1)} %get-tuple-element.56), channel_id=1, source_target_pairs={{0,14},{1,15},{2,0},{3,1},{4,2},{5,3},{6,4},{7,5},{8,6},{9,7},{10,... | collective-permute-start | bytes 737288 | tf_op jit(solution)/shard_map/ppermute | solution.py:33
  116.5 0.7 collective-permute-start.20
  117.2 1.3 collective-permute-start.23
  118.6 2.3 %shard_map.110 = (f32[8,128,512]{2,1,0:T(8,128)S(1)}, f32[8,128,512]{2,1,0:T(8,128)S(1)}) custom-call(s32[1]{0:T(128)} %bitcast.core, bf16[128,256]{1,0:T(8,128)(2,1)S(1)} %maximum_select_fusion.attended, bf16[256,8192]{1,0:T(8,128)(2,1)S(1)} %copy-done.1), custom_call_target="tpu_custom_call" | custom-call | flops 536870912 | bytes 12582912 | tf_op jit(solution)/shard_map/pallas_call | solution.py:71
  120.9 0.3 collective-permute-start.19
  121.4 1.4 collective-permute-done.30
  122.8 3.8 %collective-permute-start.31 = (bf16[80,1536]{1,0:T(8,128)(2,1)S(1)}, bf16[80,1536]{1,0:T(8,128)(2,1)S(1)}, u32[]{:S(2)}, u32[]{:S(2)}) collective-permute-start(bf16[80,1536]{1,0:T(8,128)(2,1)S(1)} %add_convert_fusion.4), channel_id=1, source_target_pairs={{0,14},{1,15},{2,0},{3,1},{4,2},{5,3},{6,4},{7,5},{8,6},{9,7},{10,... | collective-permute-start | bytes 737288 | tf_op jit(solution)/shard_map/ppermute | solution.py:33
  126.6 1.4 collective-permute-done.20
  128.1 3.8 %collective-permute-start.21 = (bf16[80,1536]{1,0:T(8,128)(2,1)S(1)}, bf16[80,1536]{1,0:T(8,128)(2,1)S(1)}, u32[]{:S(2)}, u32[]{:S(2)}) collective-permute-start(bf16[80,1536]{1,0:T(8,128)(2,1)S(1)} %add_convert_fusion.12), channel_id=1, source_target_pairs={{0,14},{1,15},{2,0},{3,1},{4,2},{5,3},{6,4},{7,5},{8,6},{9,7},{10,... | collective-permute-start | bytes 737288 | tf_op jit(solution)/shard_map/ppermute | solution.py:33
  132.2 1.1 collective-permute-done.31
  133.4 3.8 %collective-permute-start.32 = (bf16[80,1536]{1,0:T(8,128)(2,1)S(1)}, bf16[80,1536]{1,0:T(8,128)(2,1)S(1)}, u32[]{:S(2)}, u32[]{:S(2)}) collective-permute-start(bf16[80,1536]{1,0:T(8,128)(2,1)S(1)} %add_convert_fusion.3), channel_id=1, source_target_pairs={{0,14},{1,15},{2,0},{3,1},{4,2},{5,3},{6,4},{7,5},{8,6},{9,7},{10,... | collective-permute-start | bytes 737288 | tf_op jit(solution)/shard_map/ppermute | solution.py:33
  137.1 1.4 collective-permute-done.21
  138.6 3.8 %collective-permute-start.22 = (bf16[80,1536]{1,0:T(8,128)(2,1)S(1)}, bf16[80,1536]{1,0:T(8,128)(2,1)S(1)}, u32[]{:S(2)}, u32[]{:S(2)}) collective-permute-start(bf16[80,1536]{1,0:T(8,128)(2,1)S(1)} %add_convert_fusion.11), channel_id=1, source_target_pairs={{0,14},{1,15},{2,0},{3,1},{4,2},{5,3},{6,4},{7,5},{8,6},{9,7},{10,... | collective-permute-start | bytes 737288 | tf_op jit(solution)/shard_map/ppermute | solution.py:33
  142.6 1.3 collective-permute-done.32
  143.9 3.8 %collective-permute-start.33 = (bf16[80,1536]{1,0:T(8,128)(2,1)S(1)}, bf16[80,1536]{1,0:T(8,128)(2,1)S(1)}, u32[]{:S(2)}, u32[]{:S(2)}) collective-permute-start(bf16[80,1536]{1,0:T(8,128)(2,1)S(1)} %add_convert_fusion.2), channel_id=1, source_target_pairs={{0,14},{1,15},{2,0},{3,1},{4,2},{5,3},{6,4},{7,5},{8,6},{9,7},{10,... | collective-permute-start | bytes 737288 | tf_op jit(solution)/shard_map/ppermute | solution.py:33
  147.7 1.4 add_convert_fusion
  149.1 1.6 collective-permute-done.25
  150.8 3.1 %collective-permute-done.33 = bf16[80,1536]{1,0:T(8,128)(2,1)S(1)} collective-permute-done((bf16[80,1536]{1,0:T(8,128)(2,1)S(1)}, bf16[80,1536]{1,0:T(8,128)(2,1)S(1)}, u32[]{:S(2)}, u32[]{:S(2)}) %collective-permute-start.33) | collective-permute-done | bytes 245792 | tf_op jit(solution)/shard_map/ppermute | solution.py:33
  154.2 4.0 %collective-permute-done.26 = bf16[80,1536]{1,0:T(8,128)(2,1)S(1)} collective-permute-done((bf16[80,1536]{1,0:T(8,128)(2,1)S(1)}, bf16[80,1536]{1,0:T(8,128)(2,1)S(1)}, u32[]{:S(2)}, u32[]{:S(2)}) %collective-permute-start.26) | collective-permute-done | bytes 245792 | tf_op jit(solution)/shard_map/ppermute | solution.py:33
  158.2 0.8 fusion.10.first
  159.0 0.7 copy-done.30
  159.7 2.3 %shard_map.111 = bf16[32,8,1536]{2,1,0:T(8,128)(2,1)} custom-call(s32[32]{0:T(128)} %fusion.14.source, bf16[10,8,1536]{2,1,0:T(8,128)(2,1)} %fusion.10.first, bf16[10,8,1536]{2,1,0:T(8,128)(2,1)} %bitcast.22), custom_call_target="tpu_custom_call" | custom-call | bytes 1572864 | tf_op jit(solution)/shard_map/pallas_call | solution.py:304
  162.0 17.5 %all_to_all.10 = bf16[16,2,8,1536]{3,2,1,0:T(8,128)(2,1)} all-to-all(bf16[16,2,8,1536]{3,2,1,0:T(8,128)(2,1)} %bitcast.19), channel_id=1, replica_groups=mesh['dp'=16,'mp'=16] {'dp'}, dimensions={0} | all-to-all | bytes 1572864 | tf_op jit(solution)/shard_map/all_to_all | solution.py:481
  179.6 2.3 %shard_map.112 = bf16[32,8,1536]{2,1,0:T(8,128)(2,1)} custom-call(s32[32]{0:T(128)} %get-tuple-element.43.source, bf16[32,8,1536]{2,1,0:T(8,128)(2,1)} %bitcast.20), custom_call_target="tpu_custom_call" | custom-call | bytes 1572864 | tf_op jit(solution)/shard_map/pallas_call | solution.py:317
  181.9 4.1 %reduce-scatter.2.cloned.1.call-done = bf16[1,128,512]{2,1,0:T(8,128)(2,1)} async-done(((bf16[8,128,512]{2,1,0:T(8,128)(2,1)}), bf16[1,128,512]{2,1,0:T(8,128)(2,1)}) %reduce-scatter.2.cloned.1.call-update) | async-done | bytes 131088 | tf_op jit(solution)/shard_map/reduce_scatter | solution.py:474
  (112 shorter events, 2.0 us)
Async XLA Ops:
  7.2 55.5 %all-gather.2.cloned.1.call-start = ((), (), s32[]{:S(2)}) async-start(), calls=%async_computation.3 | async-start | bytes 4456448 | tf_op jit(solution)/shard_map/all_gather | solution.py:390
  10.2 20.1 %all-to-all-start = ((bf16[16,2,8,1664]{3,2,1,0:T(8,128)(2,1)}), bf16[16,2,8,1664]{3,2,1,0:T(8,128)(2,1)S(1)}, u32[]{:S(2)}, u32[]{:S(2)}) async-start(bf16[16,2,8,1664]{3,2,1,0:T(8,128)(2,1)} %bitcast.21), calls=%async_computation | async-start | bytes 1703936 | tf_op jit(solution)/shard_map/all_to_all | solution.py:391
  17.6 168.4 %reduce-scatter.2.cloned.1.call-start = ((), (), s32[]{:S(2)}) async-start(), calls=%async_computation.4 | async-start | bytes 1179648 | tf_op jit(solution)/shard_map/reduce_scatter | solution.py:474
  17.6 24.8 %collective-permute-start.2 = (bf16[1536,256]{1,0:T(8,128)(2,1)}, bf16[1536,256]{1,0:T(8,128)(2,1)S(1)}, u32[]{:S(2)}, u32[]{:S(2)}) collective-permute-start(bf16[1536,256]{1,0:T(8,128)(2,1)} %value_own.3), channel_id=1, source_target_pairs={{0,1},{1,0},{2,3},{3,2},{4,5},{5,4},{6,7},{7,6},{8,9},{9,8},{10,11... | collective-permute-start | bytes 2359304 | tf_op jit(solution)/shard_map/ppermute | solution.py:37
  30.3 1.4 copy-start.29
  33.9 1.9 collective-permute-start.3
  33.9 17.7 %collective-permute-start.4 = (bf16[80,1536]{1,0:T(8,128)(2,1)}, bf16[80,1536]{1,0:T(8,128)(2,1)S(1)}, u32[]{:S(2)}, u32[]{:S(2)}) collective-permute-start(bf16[80,1536]{1,0:T(8,128)(2,1)} %bitcast.13), channel_id=1, source_target_pairs={{0,2},{1,3},{2,4},{3,5},{4,6},{5,7},{6,8},{7,9},{8,10},{9,11},{10,... | collective-permute-start | bytes 737288 | tf_op jit(solution)/shard_map/ppermute | solution.py:33
  35.8 39.1 %copy-start.7 = (bf16[80,1536]{1,0:T(8,128)(2,1)}, bf16[80,1536]{1,0:T(8,128)(2,1)S(1)}, u32[]{:S(2)}) copy-start(bf16[80,1536]{1,0:T(8,128)(2,1)S(1)} %collective-permute-done.3.refs_1_) | copy-start | bytes 737284
  35.8 16.5 %collective-permute-start.7 = (bf16[80,1536]{1,0:T(8,128)(2,1)S(1)}, bf16[80,1536]{1,0:T(8,128)(2,1)S(1)}, u32[]{:S(2)}, u32[]{:S(2)}) collective-permute-start(bf16[80,1536]{1,0:T(8,128)(2,1)S(1)} %collective-permute-done.3.refs_1_), channel_id=1, source_target_pairs={{0,14},{1,15},{2,0},{3,1},{4,2},{5,3},{6,4},{7,5},{8,6},{9,7},{10,... | collective-permute-start | bytes 737288 | tf_op jit(solution)/shard_map/ppermute | solution.py:33
  41.4 33.5 %collective-permute-start.1 = (bf16[1536,256]{1,0:T(8,128)(2,1)}, bf16[1536,256]{1,0:T(8,128)(2,1)}, u32[]{:S(2)}, u32[]{:S(2)}) collective-permute-start(bf16[1536,256]{1,0:T(8,128)(2,1)} %key_own.1), channel_id=1, source_target_pairs={{0,1},{1,0},{2,3},{3,2},{4,5},{5,4},{6,7},{7,6},{8,9},{9,8},{10,11... | collective-permute-start | bytes 2359304 | tf_op jit(solution)/shard_map/ppermute | solution.py:37
  41.4 24.9 %collective-permute-start.6 = (bf16[80,1536]{1,0:T(8,128)(2,1)}, bf16[80,1536]{1,0:T(8,128)(2,1)S(1)}, u32[]{:S(2)}, u32[]{:S(2)}) collective-permute-start(bf16[80,1536]{1,0:T(8,128)(2,1)} %bitcast.14), channel_id=1, source_target_pairs={{0,14},{1,15},{2,0},{3,1},{4,2},{5,3},{6,4},{7,5},{8,6},{9,7},{10,... | collective-permute-start | bytes 737288 | tf_op jit(solution)/shard_map/ppermute | solution.py:33
  42.4 32.4 %copy-start.3 = (bf16[1536,256]{1,0:T(8,128)(2,1)}, bf16[1536,256]{1,0:T(8,128)(2,1)S(1)}, u32[]{:S(2)}) copy-start(bf16[1536,256]{1,0:T(8,128)(2,1)S(1)} %collective-permute-done.2.value_partner) | copy-start | bytes 2359300
  42.4 26.1 %collective-permute-start.5 = (bf16[80,1536]{1,0:T(8,128)(2,1)S(1)}, bf16[80,1536]{1,0:T(8,128)(2,1)S(1)}, u32[]{:S(2)}, u32[]{:S(2)}) collective-permute-start(bf16[80,1536]{1,0:T(8,128)(2,1)S(1)} %collective-permute-done.3.refs_1_), channel_id=1, source_target_pairs={{0,2},{1,3},{2,4},{3,5},{4,6},{5,7},{6,8},{7,9},{8,10},{9,11},{10,... | collective-permute-start | bytes 737288 | tf_op jit(solution)/shard_map/ppermute | solution.py:33
  51.6 23.3 %copy-start.10 = (bf16[80,1536]{1,0:T(8,128)(2,1)}, bf16[80,1536]{1,0:T(8,128)(2,1)S(1)}, u32[]{:S(2)}) copy-start(bf16[80,1536]{1,0:T(8,128)(2,1)S(1)} %collective-permute-done.4.refs_2_) | copy-start | bytes 737284
  51.6 16.3 %collective-permute-start.8 = (bf16[80,1536]{1,0:T(8,128)(2,1)S(1)}, bf16[80,1536]{1,0:T(8,128)(2,1)}, u32[]{:S(2)}, u32[]{:S(2)}) collective-permute-start(bf16[80,1536]{1,0:T(8,128)(2,1)S(1)} %collective-permute-done.4.refs_2_), channel_id=1, source_target_pairs={{0,2},{1,3},{2,4},{3,5},{4,6},{5,7},{6,8},{7,9},{8,10},{9,11},{10,... | collective-permute-start | bytes 737288 | tf_op jit(solution)/shard_map/ppermute | solution.py:33
  52.3 22.6 %copy-start.13 = (bf16[80,1536]{1,0:T(8,128)(2,1)}, bf16[80,1536]{1,0:T(8,128)(2,1)S(1)}, u32[]{:S(2)}) copy-start(bf16[80,1536]{1,0:T(8,128)(2,1)S(1)} %collective-permute-done.7.refs_5_) | copy-start | bytes 737284
  52.3 17.0 %collective-permute-start.11 = (bf16[80,1536]{1,0:T(8,128)(2,1)S(1)}, bf16[80,1536]{1,0:T(8,128)(2,1)}, u32[]{:S(2)}, u32[]{:S(2)}) collective-permute-start(bf16[80,1536]{1,0:T(8,128)(2,1)S(1)} %collective-permute-done.7.refs_5_), channel_id=1, source_target_pairs={{0,14},{1,15},{2,0},{3,1},{4,2},{5,3},{6,4},{7,5},{8,6},{9,7},{10,... | collective-permute-start | bytes 737288 | tf_op jit(solution)/shard_map/ppermute | solution.py:33
  62.7 9.1 %copy-start = (bf16[256,8192]{1,0:T(8,128)(2,1)S(1)}, bf16[256,8192]{1,0:T(8,128)(2,1)}, u32[]{:S(2)}) copy-start(bf16[256,8192]{1,0:T(8,128)(2,1)} %w_out.1) | copy-start | bytes 12582916
  66.3 16.1 %copy-start.2 = (bf16[1536,256]{1,0:T(8,128)(2,1)S(1)}, bf16[1536,256]{1,0:T(8,128)(2,1)}, u32[]{:S(2)}) copy-start(bf16[1536,256]{1,0:T(8,128)(2,1)} %value_own.3) | copy-start | bytes 2359300
  66.4 16.1 %copy-start.22 = (bf16[1536,256]{1,0:T(8,128)(2,1)S(1)}, bf16[1536,256]{1,0:T(8,128)(2,1)}, u32[]{:S(2)}) copy-start(bf16[1536,256]{1,0:T(8,128)(2,1)} %key_own.1) | copy-start | bytes 2359300
  66.4 16.1 %copy-start.16 = (bf16[80,1536]{1,0:T(8,128)(2,1)}, bf16[80,1536]{1,0:T(8,128)(2,1)S(1)}, u32[]{:S(2)}) copy-start(bf16[80,1536]{1,0:T(8,128)(2,1)S(1)} %collective-permute-done.6.refs_4_) | copy-start | bytes 737284
  66.4 9.0 %collective-permute-start.10 = (bf16[80,1536]{1,0:T(8,128)(2,1)S(1)}, bf16[80,1536]{1,0:T(8,128)(2,1)}, u32[]{:S(2)}, u32[]{:S(2)}) collective-permute-start(bf16[80,1536]{1,0:T(8,128)(2,1)S(1)} %collective-permute-done.6.refs_4_), channel_id=1, source_target_pairs={{0,14},{1,15},{2,0},{3,1},{4,2},{5,3},{6,4},{7,5},{8,6},{9,7},{10,... | collective-permute-start | bytes 737288 | tf_op jit(solution)/shard_map/ppermute | solution.py:33
  67.9 18.1 %collective-permute-start.12 = (bf16[80,1536]{1,0:T(8,128)(2,1)}, bf16[80,1536]{1,0:T(8,128)(2,1)}, u32[]{:S(2)}, u32[]{:S(2)}) collective-permute-start(bf16[80,1536]{1,0:T(8,128)(2,1)} %collective-permute-done.8.refs_6_), channel_id=1, source_target_pairs={{0,2},{1,3},{2,4},{3,5},{4,6},{5,7},{6,8},{7,9},{8,10},{9,11},{10,... | collective-permute-start | bytes 737288 | tf_op jit(solution)/shard_map/ppermute | solution.py:33
  68.5 14.0 %copy-start.19 = (bf16[80,1536]{1,0:T(8,128)(2,1)}, bf16[80,1536]{1,0:T(8,128)(2,1)S(1)}, u32[]{:S(2)}) copy-start(bf16[80,1536]{1,0:T(8,128)(2,1)S(1)} %collective-permute-done.5.refs_3_) | copy-start | bytes 737284
  68.5 14.0 %collective-permute-start.9 = (bf16[80,1536]{1,0:T(8,128)(2,1)S(1)}, bf16[80,1536]{1,0:T(8,128)(2,1)}, u32[]{:S(2)}, u32[]{:S(2)}) collective-permute-start(bf16[80,1536]{1,0:T(8,128)(2,1)S(1)} %collective-permute-done.5.refs_3_), channel_id=1, source_target_pairs={{0,2},{1,3},{2,4},{3,5},{4,6},{5,7},{6,8},{7,9},{8,10},{9,11},{10,... | collective-permute-start | bytes 737288 | tf_op jit(solution)/shard_map/ppermute | solution.py:33
  69.3 16.7 %collective-permute-start.15 = (bf16[80,1536]{1,0:T(8,128)(2,1)}, bf16[80,1536]{1,0:T(8,128)(2,1)}, u32[]{:S(2)}, u32[]{:S(2)}) collective-permute-start(bf16[80,1536]{1,0:T(8,128)(2,1)} %collective-permute-done.11.refs_9_), channel_id=1, source_target_pairs={{0,14},{1,15},{2,0},{3,1},{4,2},{5,3},{6,4},{7,5},{8,6},{9,7},{10,... | collective-permute-start | bytes 737288 | tf_op jit(solution)/shard_map/ppermute | solution.py:33
  74.9 14.5 %copy-start.31 = (s32[2]{0:T(128)S(1)}, s32[2]{0:T(128)}, u32[]{:S(2)}) copy-start(s32[2]{0:T(128)} %param.12) | copy-start | bytes 28
  74.9 15.0 %copy-start.6 = (bf16[10,8,1536]{2,1,0:T(8,128)(2,1)S(1)}, bf16[10,8,1536]{2,1,0:T(8,128)(2,1)}, u32[]{:S(2)}) copy-start(bf16[10,8,1536]{2,1,0:T(8,128)(2,1)} %get-tuple-element.33) | copy-start | bytes 737284
  75.0 7.5 %collective-permute-start = (bf16[64,512]{1,0:T(8,128)(2,1)S(1)}, bf16[64,512]{1,0:T(8,128)(2,1)S(1)}, u32[]{:S(2)}, u32[]{:S(2)}) collective-permute-start(bf16[64,512]{1,0:T(8,128)(2,1)S(1)} %get-tuple-element.60), channel_id=1, source_target_pairs={{0,1},{1,0},{2,3},{3,2},{4,5},{5,4},{6,7},{7,6},{8,9},{9,8},{10,11... | collective-permute-start | bytes 196616 | tf_op jit(solution)/shard_map/ppermute | solution.py:37
  75.4 23.9 %collective-permute-start.14 = (bf16[80,1536]{1,0:T(8,128)(2,1)}, bf16[80,1536]{1,0:T(8,128)(2,1)}, u32[]{:S(2)}, u32[]{:S(2)}) collective-permute-start(bf16[80,1536]{1,0:T(8,128)(2,1)} %collective-permute-done.10.refs_8_), channel_id=1, source_target_pairs={{0,14},{1,15},{2,0},{3,1},{4,2},{5,3},{6,4},{7,5},{8,6},{9,7},{10,... | collective-permute-start | bytes 737288 | tf_op jit(solution)/shard_map/ppermute | solution.py:33
  82.5 16.8 %collective-permute-start.13 = (bf16[80,1536]{1,0:T(8,128)(2,1)}, bf16[80,1536]{1,0:T(8,128)(2,1)}, u32[]{:S(2)}, u32[]{:S(2)}) collective-permute-start(bf16[80,1536]{1,0:T(8,128)(2,1)} %collective-permute-done.9.refs_7_), channel_id=1, source_target_pairs={{0,2},{1,3},{2,4},{3,5},{4,6},{5,7},{6,8},{7,9},{8,10},{9,11},{10,... | collective-permute-start | bytes 737288 | tf_op jit(solution)/shard_map/ppermute | solution.py:33
  82.5 1.1 copy-start.4
  86.0 13.3 %collective-permute-start.16 = (bf16[80,1536]{1,0:T(8,128)(2,1)}, bf16[80,1536]{1,0:T(8,128)(2,1)}, u32[]{:S(2)}, u32[]{:S(2)}) collective-permute-start(bf16[80,1536]{1,0:T(8,128)(2,1)} %collective-permute-done.12.refs_0_.refs_10_), channel_id=1, source_target_pairs={{0,2},{1,3},{2,4},{3,5},{4,6},{5,7},{6,8},{7,9},{8,10},{9,11},{10,... | collective-permute-start | bytes 737288 | tf_op jit(solution)/shard_map/ppermute | solution.py:33
  86.3 13.0 %collective-permute-start.17 = (bf16[80,1536]{1,0:T(8,128)(2,1)}, bf16[80,1536]{1,0:T(8,128)(2,1)}, u32[]{:S(2)}, u32[]{:S(2)}) collective-permute-start(bf16[80,1536]{1,0:T(8,128)(2,1)} %collective-permute-done.15.refs_3_.refs_13_), channel_id=1, source_target_pairs={{0,14},{1,15},{2,0},{3,1},{4,2},{5,3},{6,4},{7,5},{8,6},{9,7},{10,... | collective-permute-start | bytes 737288 | tf_op jit(solution)/shard_map/ppermute | solution.py:33
  90.0 0.9 copy-start.8
  90.9 0.9 copy-start.11
  99.2 9.1 %copy-start.5 = (bf16[1536,256]{1,0:T(8,128)(2,1)S(1)}, bf16[1536,256]{1,0:T(8,128)(2,1)}, u32[]{:S(2)}) copy-start(bf16[1536,256]{1,0:T(8,128)(2,1)} %copy-done.3) | copy-start | bytes 2359300
  99.2 9.1 %copy-start.9 = (bf16[80,1536]{1,0:T(8,128)(2,1)S(1)}, bf16[80,1536]{1,0:T(8,128)(2,1)}, u32[]{:S(2)}) copy-start(bf16[80,1536]{1,0:T(8,128)(2,1)} %copy-done.7) | copy-start | bytes 737284
  99.2 9.1 %copy-start.12 = (bf16[80,1536]{1,0:T(8,128)(2,1)S(1)}, bf16[80,1536]{1,0:T(8,128)(2,1)}, u32[]{:S(2)}) copy-start(bf16[80,1536]{1,0:T(8,128)(2,1)} %copy-done.10) | copy-start | bytes 737284
  99.2 9.1 %copy-start.15 = (bf16[80,1536]{1,0:T(8,128)(2,1)S(1)}, bf16[80,1536]{1,0:T(8,128)(2,1)}, u32[]{:S(2)}) copy-start(bf16[80,1536]{1,0:T(8,128)(2,1)} %copy-done.13) | copy-start | bytes 737284
  99.2 9.1 %copy-start.18 = (bf16[80,1536]{1,0:T(8,128)(2,1)S(1)}, bf16[80,1536]{1,0:T(8,128)(2,1)}, u32[]{:S(2)}) copy-start(bf16[80,1536]{1,0:T(8,128)(2,1)} %copy-done.16) | copy-start | bytes 737284
  99.2 9.1 %copy-start.21 = (bf16[80,1536]{1,0:T(8,128)(2,1)S(1)}, bf16[80,1536]{1,0:T(8,128)(2,1)}, u32[]{:S(2)}) copy-start(bf16[80,1536]{1,0:T(8,128)(2,1)} %copy-done.19) | copy-start | bytes 737284
  108.2 10.3 %copy-start.25 = (bf16[80,1536]{1,0:T(8,128)(2,1)}, bf16[80,1536]{1,0:T(8,128)(2,1)S(1)}, u32[]{:S(2)}) copy-start(bf16[80,1536]{1,0:T(8,128)(2,1)S(1)} %get-tuple-element.44) | copy-start | bytes 737284
  108.2 10.3 %copy-start.1 = (bf16[256,8192]{1,0:T(8,128)(2,1)S(1)}, bf16[256,8192]{1,0:T(8,128)(2,1)}, u32[]{:S(2)}) copy-start(bf16[256,8192]{1,0:T(8,128)(2,1)} %w_out.1) | copy-start | bytes 12582916
  108.2 13.0 %collective-permute-start.27 = (bf16[80,1536]{1,0:T(8,128)(2,1)S(1)}, bf16[80,1536]{1,0:T(8,128)(2,1)S(1)}, u32[]{:S(2)}, u32[]{:S(2)}) collective-permute-start(bf16[80,1536]{1,0:T(8,128)(2,1)S(1)} %get-tuple-element.53), channel_id=1, source_target_pairs={{0,2},{1,3},{2,4},{3,5},{4,6},{5,7},{6,8},{7,9},{8,10},{9,11},{10,... | collective-permute-start | bytes 737288 | tf_op jit(solution)/shard_map/ppermute | solution.py:33
  112.7 5.8 %collective-permute-start.18 = (bf16[64,256]{1,0:T(8,128)(2,1)S(1)}, bf16[64,256]{1,0:T(8,128)(2,1)S(1)}, u32[]{:S(2)}, u32[]{:S(2)}) collective-permute-start(bf16[64,256]{1,0:T(8,128)(2,1)S(1)} %get-tuple-element.40), channel_id=1, source_target_pairs={{0,1},{1,0},{2,3},{3,2},{4,5},{5,4},{6,7},{7,6},{8,9},{9,8},{10,11... | collective-permute-start | bytes 98312 | tf_op jit(solution)/shard_map/ppermute | solution.py:37
  113.4 9.3 %collective-permute-start.30 = (bf16[80,1536]{1,0:T(8,128)(2,1)S(1)}, bf16[80,1536]{1,0:T(8,128)(2,1)S(1)}, u32[]{:S(2)}, u32[]{:S(2)}) collective-permute-start(bf16[80,1536]{1,0:T(8,128)(2,1)S(1)} %get-tuple-element.56), channel_id=1, source_target_pairs={{0,14},{1,15},{2,0},{3,1},{4,2},{5,3},{6,4},{7,5},{8,6},{9,7},{10,... | collective-permute-start | bytes 737288 | tf_op jit(solution)/shard_map/ppermute | solution.py:33
  116.5 11.5 %collective-permute-start.20 = (bf16[80,1536]{1,0:T(8,128)(2,1)S(1)}, bf16[80,1536]{1,0:T(8,128)(2,1)S(1)}, u32[]{:S(2)}, u32[]{:S(2)}) collective-permute-start(bf16[80,1536]{1,0:T(8,128)(2,1)S(1)} %get-tuple-element.45), channel_id=1, source_target_pairs={{0,14},{1,15},{2,0},{3,1},{4,2},{5,3},{6,4},{7,5},{8,6},{9,7},{10,... | collective-permute-start | bytes 737288 | tf_op jit(solution)/shard_map/ppermute | solution.py:33
  117.2 14.6 %collective-permute-start.23 = (bf16[80,1536]{1,0:T(8,128)(2,1)S(1)}, bf16[80,1536]{1,0:T(8,128)(2,1)S(1)}, u32[]{:S(2)}, u32[]{:S(2)}) collective-permute-start(bf16[80,1536]{1,0:T(8,128)(2,1)S(1)} %get-tuple-element.48), channel_id=1, source_target_pairs={{0,2},{1,3},{2,4},{3,5},{4,6},{5,7},{6,8},{7,9},{8,10},{9,11},{10,... | collective-permute-start | bytes 737288 | tf_op jit(solution)/shard_map/ppermute | solution.py:33
  120.9 26.8 %collective-permute-start.19 = (f32[8,128,512]{2,1,0:T(8,128)S(1)}, f32[8,128,512]{2,1,0:T(8,128)S(1)}, u32[]{:S(2)}, u32[]{:S(2)}) collective-permute-start(f32[8,128,512]{2,1,0:T(8,128)S(1)} %get-tuple-element.42), channel_id=1, source_target_pairs={{0,1},{1,0},{2,3},{3,2},{4,5},{5,4},{6,7},{7,6},{8,9},{9,8},{10,11... | collective-permute-start | bytes 6291464 | tf_op jit(solution)/shard_map/ppermute | solution.py:37
  121.3 10.7 %collective-permute-start.28 = (bf16[80,1536]{1,0:T(8,128)(2,1)S(1)}, bf16[80,1536]{1,0:T(8,128)(2,1)S(1)}, u32[]{:S(2)}, u32[]{:S(2)}) collective-permute-start(bf16[80,1536]{1,0:T(8,128)(2,1)S(1)} %add_convert_fusion.6), channel_id=1, source_target_pairs={{0,2},{1,3},{2,4},{3,5},{4,6},{5,7},{6,8},{7,9},{8,10},{9,11},{10,... | collective-permute-start | bytes 737288 | tf_op jit(solution)/shard_map/ppermute | solution.py:33
  122.8 10.5 %collective-permute-start.31 = (bf16[80,1536]{1,0:T(8,128)(2,1)S(1)}, bf16[80,1536]{1,0:T(8,128)(2,1)S(1)}, u32[]{:S(2)}, u32[]{:S(2)}) collective-permute-start(bf16[80,1536]{1,0:T(8,128)(2,1)S(1)} %add_convert_fusion.4), channel_id=1, source_target_pairs={{0,14},{1,15},{2,0},{3,1},{4,2},{5,3},{6,4},{7,5},{8,6},{9,7},{10,... | collective-permute-start | bytes 737288 | tf_op jit(solution)/shard_map/ppermute | solution.py:33
  128.1 10.5 %collective-permute-start.21 = (bf16[80,1536]{1,0:T(8,128)(2,1)S(1)}, bf16[80,1536]{1,0:T(8,128)(2,1)S(1)}, u32[]{:S(2)}, u32[]{:S(2)}) collective-permute-start(bf16[80,1536]{1,0:T(8,128)(2,1)S(1)} %add_convert_fusion.12), channel_id=1, source_target_pairs={{0,14},{1,15},{2,0},{3,1},{4,2},{5,3},{6,4},{7,5},{8,6},{9,7},{10,... | collective-permute-start | bytes 737288 | tf_op jit(solution)/shard_map/ppermute | solution.py:33
  131.9 10.5 %collective-permute-start.24 = (bf16[80,1536]{1,0:T(8,128)(2,1)S(1)}, bf16[80,1536]{1,0:T(8,128)(2,1)S(1)}, u32[]{:S(2)}, u32[]{:S(2)}) collective-permute-start(bf16[80,1536]{1,0:T(8,128)(2,1)S(1)} %add_convert_fusion.10), channel_id=1, source_target_pairs={{0,2},{1,3},{2,4},{3,5},{4,6},{5,7},{6,8},{7,9},{8,10},{9,11},{10,... | collective-permute-start | bytes 737288 | tf_op jit(solution)/shard_map/ppermute | solution.py:33
  132.1 18.7 %collective-permute-start.29 = (bf16[80,1536]{1,0:T(8,128)(2,1)S(1)}, bf16[80,1536]{1,0:T(8,128)(2,1)S(1)}, u32[]{:S(2)}, u32[]{:S(2)}) collective-permute-start(bf16[80,1536]{1,0:T(8,128)(2,1)S(1)} %add_convert_fusion.5), channel_id=1, source_target_pairs={{0,2},{1,3},{2,4},{3,5},{4,6},{5,7},{6,8},{7,9},{8,10},{9,11},{10,... | collective-permute-start | bytes 737288 | tf_op jit(solution)/shard_map/ppermute | solution.py:33
  133.4 10.5 %collective-permute-start.32 = (bf16[80,1536]{1,0:T(8,128)(2,1)S(1)}, bf16[80,1536]{1,0:T(8,128)(2,1)S(1)}, u32[]{:S(2)}, u32[]{:S(2)}) collective-permute-start(bf16[80,1536]{1,0:T(8,128)(2,1)S(1)} %add_convert_fusion.3), channel_id=1, source_target_pairs={{0,14},{1,15},{2,0},{3,1},{4,2},{5,3},{6,4},{7,5},{8,6},{9,7},{10,... | collective-permute-start | bytes 737288 | tf_op jit(solution)/shard_map/ppermute | solution.py:33
  138.6 12.1 %copy-start.24 = (bf16[80,1536]{1,0:T(8,128)(2,1)S(1)}, bf16[80,1536]{1,0:T(8,128)(2,1)}, u32[]{:S(2)}) copy-start(bf16[80,1536]{1,0:T(8,128)(2,1)} %copy-done.23) | copy-start | bytes 737284
  138.6 15.5 %collective-permute-start.22 = (bf16[80,1536]{1,0:T(8,128)(2,1)S(1)}, bf16[80,1536]{1,0:T(8,128)(2,1)S(1)}, u32[]{:S(2)}, u32[]{:S(2)}) collective-permute-start(bf16[80,1536]{1,0:T(8,128)(2,1)S(1)} %add_convert_fusion.11), channel_id=1, source_target_pairs={{0,14},{1,15},{2,0},{3,1},{4,2},{5,3},{6,4},{7,5},{8,6},{9,7},{10,... | collective-permute-start | bytes 737288 | tf_op jit(solution)/shard_map/ppermute | solution.py:33
  142.4 11.6 %copy-start.28 = (bf16[80,1536]{1,0:T(8,128)(2,1)S(1)}, bf16[80,1536]{1,0:T(8,128)(2,1)}, u32[]{:S(2)}) copy-start(bf16[80,1536]{1,0:T(8,128)(2,1)} %copy-done.27) | copy-start | bytes 737284
  142.5 8.2 %collective-permute-start.25 = (bf16[80,1536]{1,0:T(8,128)(2,1)S(1)}, bf16[80,1536]{1,0:T(8,128)(2,1)S(1)}, u32[]{:S(2)}, u32[]{:S(2)}) collective-permute-start(bf16[80,1536]{1,0:T(8,128)(2,1)S(1)} %add_convert_fusion.9), channel_id=1, source_target_pairs={{0,2},{1,3},{2,4},{3,5},{4,6},{5,7},{6,8},{7,9},{8,10},{9,11},{10,... | collective-permute-start | bytes 737288 | tf_op jit(solution)/shard_map/ppermute | solution.py:33
  143.9 14.3 %copy-start.26 = (bf16[80,1536]{1,0:T(8,128)(2,1)S(1)}, bf16[80,1536]{1,0:T(8,128)(2,1)}, u32[]{:S(2)}) copy-start(bf16[80,1536]{1,0:T(8,128)(2,1)} %copy-done.25) | copy-start | bytes 737284
  143.9 10.1 %collective-permute-start.33 = (bf16[80,1536]{1,0:T(8,128)(2,1)S(1)}, bf16[80,1536]{1,0:T(8,128)(2,1)S(1)}, u32[]{:S(2)}, u32[]{:S(2)}) collective-permute-start(bf16[80,1536]{1,0:T(8,128)(2,1)S(1)} %add_convert_fusion.2), channel_id=1, source_target_pairs={{0,14},{1,15},{2,0},{3,1},{4,2},{5,3},{6,4},{7,5},{8,6},{9,7},{10,... | collective-permute-start | bytes 737288 | tf_op jit(solution)/shard_map/ppermute | solution.py:33
  150.7 7.5 %collective-permute-start.26 = (bf16[80,1536]{1,0:T(8,128)(2,1)S(1)}, bf16[80,1536]{1,0:T(8,128)(2,1)S(1)}, u32[]{:S(2)}, u32[]{:S(2)}) collective-permute-start(bf16[80,1536]{1,0:T(8,128)(2,1)S(1)} %add_convert_fusion.8), channel_id=1, source_target_pairs={{0,2},{1,3},{2,4},{3,5},{4,6},{5,7},{6,8},{7,9},{8,10},{9,11},{10,... | collective-permute-start | bytes 737288 | tf_op jit(solution)/shard_map/ppermute | solution.py:33
  154.1 4.9 %collective-permute-start.34 = (bf16[80,1536]{1,0:T(8,128)(2,1)S(1)}, bf16[80,1536]{1,0:T(8,128)(2,1)S(1)}, u32[]{:S(2)}, u32[]{:S(2)}) collective-permute-start(bf16[80,1536]{1,0:T(8,128)(2,1)S(1)} %add_convert_fusion.1), channel_id=1, source_target_pairs={{0,1},{1,0},{2,3},{3,2},{4,5},{5,4},{6,7},{7,6},{8,9},{9,8},{10,11... | collective-permute-start | bytes 737288 | tf_op jit(solution)/shard_map/ppermute | solution.py:37
  (6 other events, 4.9 us)
Sparse Core Ops, SparseCore 0:
  10.3 52.3 all-gather.1
  149.2 36.7 reduce-scatter.1
where the time goes:
time: 194 us; the launch traced here: 193 us
  starting transfers between devices  57.3 us (30%)
  waiting for transfers between devices  52.2 us (27%)
  Pallas kernels  30.8 us (16%)
  blocking collectives  17.5 us (9%)
  between operations  14.6 us (8%)
  local copies, waits for them, and re-layouts  8.59 us (4%)
  matrix products  6.8 us (4%)
  other arithmetic  4.92 us (3%)
    ppermute x28, starting transfers between devices, chip_shift(): return lax.ppermute(value, 'mp', pairs)  49 us
    ppermute x28, waiting for transfers between devices, chip_shift(): return lax.ppermute(value, 'mp', pairs)  28.9 us
    all_to_all x1, blocking collectives, per_device(): lax.all_to_all(join_pick(*scattered, returns).reshape(groups, capacity, r...  17.5 us
    all_to_all x1, waiting for transfers between devices, per_device(): lax.all_to_all(send_rows.reshape(groups, capacity, rows_dev, enc_width +...  12.5 us
    unnamed x64, local copies, waits for them, and re-layouts  8.04 us
    pallas_call x1, Pallas kernels, make_softmax(): pl.pallas_call(functools.partial(softmax_kernel, scale, per_slot, period,...  7.55 us
    all_to_all x1, starting transfers between devices, per_device(): lax.all_to_all(send_rows.reshape(groups, capacity, rows_dev, enc_width +...  7.4 us
    all_gather x1, waiting for transfers between devices, per_device(): both = lax.all_gather(both, 'mp', axis=1, tiled=True)  6.66 us
  transfers between devices with their start and end apart: 38, of which 15 were waited for; matrix products, arithmetic and copies ran while one was open for 6% of the time, Pallas kernels for 11%

commit v1 on v0

--- a/solution.py
+++ b/solution.py
@@ -164,7 +164,7 @@
     )(lines, *chunks)
 
 
-def softmax_kernel(scale, per_slot, period, late, count, lines, early, *refs):
+def softmax_kernel(scale, per_slot, period, late, core, counts, lines, early, *refs):
     keys, last, *columns_refs = refs[-4:]
     weights_out, grads_out = refs[late : late + 2], refs[late + 2 : -4]
     gather(refs[:late], keys)
@@ -174,7 +174,7 @@
     scores = []
     for product in both:
         columns = lax.broadcasted_iota(jnp.int32, (middle, product.shape[1]), 1)
-        live = (columns % period) // per_slot < count[0]
+        live = (columns % period) // per_slot < counts[core[0]]
         score = (product[:middle] + product[2 * middle :]) * scale
         scores.append(jnp.where(live, score, -jnp.inf))
     peak = functools.reduce(
@@ -210,7 +210,7 @@
                 place += 1
 
 
-def make_softmax(count, lines, early, chunks, per_slot, shapes, scale):
+def make_softmax(core, counts, lines, early, chunks, per_slot, shapes, scale):
     rows, enc = lines.shape
     late = sum(c.shape[0] for c in chunks)
     keys = early.shape[1] + late
@@ -222,7 +222,7 @@
             jax.ShapeDtypeStruct((rows // 3, late), BF),
         ]
         + [jax.ShapeDtypeStruct((n, enc), kind) for n, kind in shapes],
-        in_specs=[pl.BlockSpec(memory_space=pltpu.SMEM)] + in_vmem(2 + len(chunks)),
+        in_specs=[pl.BlockSpec(memory_space=pltpu.SMEM)] * 2 + in_vmem(2 + len(chunks)),
         out_specs=in_vmem(2 + len(shapes)),
         scratch_shapes=[
             pltpu.VMEM((late, enc), BF),
@@ -236,7 +236,7 @@
             bytes_accessed=2 * enc * (rows + late + 2 * keys) + 4 * rows * keys,
             transcendentals=rows * keys // 2,
         ),
-    )(count, lines, early, *chunks)
+    )(core, counts, lines, early, *chunks)
 
 
 def attended_kernel(first, second, value_own, value_partner, *refs):
@@ -289,27 +289,29 @@
             outs[k][i] = jnp.where(index >= 0, value, jnp.zeros_like(value))
 
 
-def join_kernel(source, first, second, out):
+def join_kernel(core, source, first, second, out):
     split = first.shape[0]
 
     @pl.loop(0, out.shape[0])
     def _(i):
-        low = jnp.minimum(jnp.maximum(source[i], 0), split - 1)
-        high = jnp.maximum(source[i] - split, 0)
-        out[i] = jnp.where(source[i] < split, first[low], second[high])
-
-
-def join_pick(first, second, source):
+        slot = jnp.maximum(source[i], 0)
+        place = jnp.where(core[0] == 0, slot, (slot + split) % (2 * split))
+        low = jnp.minimum(place, split - 1)
+        high = jnp.maximum(place - split, 0)
+        out[i] = jnp.where(place < split, first[low], second[high])
+
+
+def join_pick(first, second, source, core):
     shape = (source.shape[0],) + first.shape[1:]
     return pl.pallas_call(
         join_kernel,
         out_shape=jax.ShapeDtypeStruct(shape, BF),
-        in_specs=[pl.BlockSpec(memory_space=pltpu.SMEM)] + in_vmem(2),
+        in_specs=[pl.BlockSpec(memory_space=pltpu.SMEM)] * 2 + in_vmem(2),
         out_specs=in_vmem(1)[0],
         cost_estimate=pl.CostEstimate(
             flops=0, bytes_accessed=4 * math.prod(shape), transcendentals=0
         ),
-    )(source.astype(jnp.int32), first, second)
+    )(core, source, first, second)
 
 
 def pick(rows, source, width=None, parts=1):
@@ -400,7 +402,6 @@
     wanted = (slots + core * MAXN) % slots_group
     matches = local_slot[None, :] == wanted[:, None]
     chosen = jnp.sum(jnp.where(matches, slot_order[None, :] + 1, 0), axis=1) - 1
-    returns = jnp.maximum(jnp.where(core == 0, local_slot, (local_slot + MAXN) % slots_group), 0)
     chunk_rows = MAXN * rows_dev
     kept, given = pick(got, chosen, enc_width, spans)
     kept, given = kept.reshape(chunk_rows, enc_width), given.reshape(chunk_rows, enc_width)
@@ -425,10 +426,10 @@
     first_late = 2 + 4 * (reach - 2)
     early, late = keys[:first_late], keys[first_late:]
 
-    count = lax.dynamic_slice_in_dim(counts, core, 1)
     shapes = [(chunk_rows, BF)] * len(keys)
     outs = make_softmax(
-        count,
+        core.reshape(1),
+        counts,
         lines,
         make_products(lines, early),
         late,
@@ -479,7 +480,7 @@
     )
 
     returned = lax.all_to_all(
-        join_pick(*scattered, returns).reshape(groups, capacity, rows_dev, enc_width),
+        join_pick(*scattered, local_slot, core.reshape(1)).reshape(groups, capacity, rows_dev, enc_width),
         "dp",
         split_axis=0,
         concat_axis=0,

time: 194 us -> 187 us (0.964)
  Pallas kernels: 30.8 us -> 25.9 us
  local copies, waits for them, and re-layouts: 8.59 us -> 4.29 us
    unnamed x64 -> x54, local copies, waits for them, and re-layouts: 8.04 us -> 4.29 us
    ppermute x28, waiting for transfers between devices: 28.9 us -> 32.2 us  [chip_shift(): return lax.ppermute(value, 'mp', pairs)]
  transfers between devices with their start and end apart: 38 -> 38, of which waited for: 15 -> 15; matrix products, arithmetic and copies ran while one was open for 6% -> 7% of each run, Pallas kernels for 11% -> 9%
where the time goes in v1:
time: 187 us; the launch traced here: 186 us
  starting transfers between devices  57.2 us (31%)
  waiting for transfers between devices  54.1 us (29%)
  Pallas kernels  25.9 us (14%)
  blocking collectives  17.4 us (9%)
  between operations  14.6 us (8%)
  matrix products  6.8 us (4%)
  other arithmetic  6.15 us (3%)
  local copies, waits for them, and re-layouts  4.29 us (2%)
    ppermute x28, starting transfers between devices, chip_shift(): return lax.ppermute(value, 'mp', pairs)  48.7 us
    ppermute x28, waiting for transfers between devices, chip_shift(): return lax.ppermute(value, 'mp', pairs)  32.2 us
    all_to_all x1, blocking collectives, per_device(): lax.all_to_all(join_pick(*scattered, local_slot, core.reshape(1)).reshape...  17.4 us
    all_to_all x1, waiting for transfers between devices, per_device(): lax.all_to_all(send_rows.reshape(groups, capacity, rows_dev, enc_width +...  12.5 us
    all_to_all x1, starting transfers between devices, per_device(): lax.all_to_all(send_rows.reshape(groups, capacity, rows_dev, enc_width +...  7.54 us
    pallas_call x1, Pallas kernels, make_softmax(): pl.pallas_call(functools.partial(softmax_kernel, scale, per_slot, period,...  6.61 us
    all_gather x1, waiting for transfers between devices, per_device(): both = lax.all_gather(both, 'mp', axis=1, tiled=True)  5.9 us
    pallas_call x2, Pallas kernels, pick(): pl.pallas_call(functools.partial(pick_kernel, parts), out_shape=[jax.Shap...  4.48 us
  transfers between devices with their start and end apart: 38, of which 15 were waited for; matrix products, arithmetic and copies ran while one was open for 7% of the time, Pallas kernels for 9%

profile of v1, /device:TPU:2, one launch (start us, length us, event | category | flops | bytes accessed | tf_op | source)
XLA Modules:
  0.0 186.4 jit_solution(13035772117454367554)
XLA Ops:
  7.2 2.9 %shard_map.104 = (bf16[32,8,1664]{2,1,0:T(8,128)(2,1)}, s32[32]{0:T(128)}, bf16[256,512]{1,0:T(8,128)(2,1)}) custom-call(s32[32]{0:T(128)} %owner.1, bf16[32,8,1536]{2,1,0:T(8,128)(2,1)} %rows.1, bf16[128,512]{1,0:T(8,128)(2,1)} %hidden.1, bf16[128,512]{1,0:T(8,128)(2,1)} %grad.1), custom_call_target="tpu_custom_call" | custom-call | bytes 1572864 | tf_op jit(solution)/shard_map/pallas_call | solution.py:357
  10.1 7.5 %all-to-all-start = ((bf16[16,2,8,1664]{3,2,1,0:T(8,128)(2,1)}), bf16[16,2,8,1664]{3,2,1,0:T(8,128)(2,1)S(1)}, u32[]{:S(2)}, u32[]{:S(2)}) async-start(bf16[16,2,8,1664]{3,2,1,0:T(8,128)(2,1)} %bitcast.21), calls=%async_computation | async-start | bytes 1703936 | tf_op jit(solution)/shard_map/all_to_all | solution.py:393
  17.7 0.1 collective-permute-start.2
  17.8 12.5 %all-to-all-done = bf16[16,2,8,1664]{3,2,1,0:T(8,128)(2,1)S(1)} async-done(((bf16[16,2,8,1664]{3,2,1,0:T(8,128)(2,1)}), bf16[16,2,8,1664]{3,2,1,0:T(8,128)(2,1)S(1)}, u32[]{:S(2)}, u32[]{:S(2)}) %all-to-all-start) | async-done | bytes 852000 | tf_op jit(solution)/shard_map/all_to_all | solution.py:393
  30.3 0.7 fusion.13.source
  31.0 0.6 copy-done.26
  31.6 0.2 select_reduce_fusion
  31.8 0.5 broadcast_add_fusion.source
  32.3 2.2 %shard_map.106 = (bf16[10,8,1536]{2,1,0:T(8,128)(2,1)}, bf16[10,8,1536]{2,1,0:T(8,128)(2,1)}) custom-call(s32[20]{0:T(128)} %broadcast_add_fusion.source, bf16[32,8,1664]{2,1,0:T(8,128)(2,1)} %bitcast.18), custom_call_target="tpu_custom_call" | custom-call | bytes 983040 | tf_op jit(solution)/shard_map/pallas_call | solution.py:319
  34.5 1.9 %collective-permute-start.4 = (bf16[80,1536]{1,0:T(8,128)(2,1)}, bf16[80,1536]{1,0:T(8,128)(2,1)S(1)}, u32[]{:S(2)}, u32[]{:S(2)}) collective-permute-start(bf16[80,1536]{1,0:T(8,128)(2,1)} %bitcast.13), channel_id=1, source_target_pairs={{0,2},{1,3},{2,4},{3,5},{4,6},{5,7},{6,8},{7,9},{8,10},{9,11},{10,... | collective-permute-start | bytes 737288 | tf_op jit(solution)/shard_map/ppermute | solution.py:33
  36.4 5.6 %collective-permute-start.7 = (bf16[80,1536]{1,0:T(8,128)(2,1)S(1)}, bf16[80,1536]{1,0:T(8,128)(2,1)S(1)}, u32[]{:S(2)}, u32[]{:S(2)}) collective-permute-start(bf16[80,1536]{1,0:T(8,128)(2,1)S(1)} %collective-permute-done.3.refs_1_), channel_id=1, source_target_pairs={{0,14},{1,15},{2,0},{3,1},{4,2},{5,3},{6,4},{7,5},{8,6},{9,7},{10,... | collective-permute-start | bytes 737288 | tf_op jit(solution)/shard_map/ppermute | solution.py:33
  42.0 1.0 collective-permute-start.6
  43.1 1.0 collective-permute-start.5
  44.1 8.0 %collective-permute-done.4.refs_2_ = bf16[80,1536]{1,0:T(8,128)(2,1)S(1)} collective-permute-done((bf16[80,1536]{1,0:T(8,128)(2,1)}, bf16[80,1536]{1,0:T(8,128)(2,1)S(1)}, u32[]{:S(2)}, u32[]{:S(2)}) %collective-permute-start.4) | collective-permute-done | bytes 245792 | tf_op jit(solution)/shard_map/ppermute | solution.py:33
  52.1 1.2 collective-permute-done.7.refs_5_
  53.4 3.7 %collective-permute-start.11 = (bf16[80,1536]{1,0:T(8,128)(2,1)S(1)}, bf16[80,1536]{1,0:T(8,128)(2,1)S(1)}, u32[]{:S(2)}, u32[]{:S(2)}) collective-permute-start(bf16[80,1536]{1,0:T(8,128)(2,1)S(1)} %collective-permute-done.7.refs_5_), channel_id=1, source_target_pairs={{0,14},{1,15},{2,0},{3,1},{4,2},{5,3},{6,4},{7,5},{8,6},{9,7},{10,... | collective-permute-start | bytes 737288 | tf_op jit(solution)/shard_map/ppermute | solution.py:33
  57.1 5.9 %all-gather.2.cloned.1.call-done = bf16[256,8192]{1,0:T(8,128)(2,1)} async-done(((bf16[256,512]{1,0:T(8,128)(2,1)}), bf16[256,8192]{1,0:T(8,128)(2,1)}) %all-gather.2.cloned.1.call-update) | async-done | bytes 4194320 | tf_op jit(solution)/shard_map/all_gather | solution.py:392
  63.0 3.7 %fusion.4 = bf16[128,256]{1,0:T(8,128)(2,1)S(1)} fusion(bf16[8192,256]{1,0:T(8,128)(2,1)} %param.14, bf16[256,8192]{1,0:T(8,128)(2,1)} %all-gather.2.cloned.1.call-done), kind=kOutput, calls=%fused_computation.5 | convolution fusion | flops 536903680 | bytes 6356992 | tf_op jit(solution)/shard_map/dot_general | solution.py:20
  66.7 1.5 collective-permute-start.10
  68.2 0.6 collective-permute-start.12
  68.8 0.6 collective-permute-start.9
  69.4 2.6 %collective-permute-start.15 = (bf16[80,1536]{1,0:T(8,128)(2,1)S(1)}, bf16[80,1536]{1,0:T(8,128)(2,1)S(1)}, u32[]{:S(2)}, u32[]{:S(2)}) collective-permute-start(bf16[80,1536]{1,0:T(8,128)(2,1)S(1)} %collective-permute-done.11.refs_9_), channel_id=1, source_target_pairs={{0,14},{1,15},{2,0},{3,1},{4,2},{5,3},{6,4},{7,5},{8,6},{9,7},{10,... | collective-permute-start | bytes 737288 | tf_op jit(solution)/shard_map/ppermute | solution.py:33
  72.0 3.1 %fusion.7 = bf16[128,256]{1,0:T(8,128)(2,1)S(1)} fusion(bf16[256,8192]{1,0:T(8,128)(2,1)S(1)} %copy-done, bf16[256,8192]{1,0:T(8,128)(2,1)} %all-gather.2.cloned.1.call-done), kind=kOutput, calls=%fused_computation.6 | convolution fusion | flops 536903680 | bytes 6356992 | tf_op jit(solution)/shard_map/dot_general | solution.py:24
  75.2 0.3 collective-permute-start
  75.5 2.6 %collective-permute-start.14 = (bf16[80,1536]{1,0:T(8,128)(2,1)S(1)}, bf16[80,1536]{1,0:T(8,128)(2,1)S(1)}, u32[]{:S(2)}, u32[]{:S(2)}) collective-permute-start(bf16[80,1536]{1,0:T(8,128)(2,1)S(1)} %collective-permute-done.10.refs_8_), channel_id=1, source_target_pairs={{0,14},{1,15},{2,0},{3,1},{4,2},{5,3},{6,4},{7,5},{8,6},{9,7},{10,... | collective-permute-start | bytes 737288 | tf_op jit(solution)/shard_map/ppermute | solution.py:33
  78.2 4.3 %collective-permute-done.9.refs_7_ = bf16[80,1536]{1,0:T(8,128)(2,1)S(1)} collective-permute-done((bf16[80,1536]{1,0:T(8,128)(2,1)S(1)}, bf16[80,1536]{1,0:T(8,128)(2,1)S(1)}, u32[]{:S(2)}, u32[]{:S(2)}) %collective-permute-start.9) | collective-permute-done | bytes 245792 | tf_op jit(solution)/shard_map/ppermute | solution.py:33
  82.5 1.2 shard_map.105.lines
  83.7 0.1 collective-permute-start.16
  83.8 3.3 %collective-permute-start.17 = (bf16[80,1536]{1,0:T(8,128)(2,1)S(1)}, bf16[80,1536]{1,0:T(8,128)(2,1)S(1)}, u32[]{:S(2)}, u32[]{:S(2)}) collective-permute-start(bf16[80,1536]{1,0:T(8,128)(2,1)S(1)} %collective-permute-done.15.refs_3_.refs_13_), channel_id=1, source_target_pairs={{0,14},{1,15},{2,0},{3,1},{4,2},{5,3},{6,4},{7,5},{8,6},{9,7},{10,... | collective-permute-start | bytes 737288 | tf_op jit(solution)/shard_map/ppermute | solution.py:33
  87.1 3.2 %shard_map.107.early = f32[768,800]{1,0:T(8,128)S(1)} custom-call(bf16[768,1536]{1,0:T(8,128)(2,1)S(1)} %shard_map.105.lines, bf16[80,1536]{1,0:T(8,128)(2,1)S(1)} %bitcast.15, bf16[80,1536]{1,0:T(8,128)(2,1)S(1)} %collective-permute-done.3.refs_1_, bf16[80,1536]{1,0:T(8,128)(2,1)S(1)} %collective-permute-done.4.refs_2_, ...), custom_call_target="tpu_custom_call" | custom-call | flops 1887436800 | bytes 7274496 | tf_op jit(solution)/shard_map/pallas_call | solution.py:152
  90.3 2.3 %collective-permute-done.13.refs_1_.refs_11_ = bf16[80,1536]{1,0:T(8,128)(2,1)S(1)} collective-permute-done((bf16[80,1536]{1,0:T(8,128)(2,1)S(1)}, bf16[80,1536]{1,0:T(8,128)(2,1)S(1)}, u32[]{:S(2)}, u32[]{:S(2)}) %collective-permute-start.13) | collective-permute-done | bytes 245792 | tf_op jit(solution)/shard_map/ppermute | solution.py:33
  92.6 3.3 %collective-permute-done.16.refs_4_.refs_14_ = bf16[80,1536]{1,0:T(8,128)(2,1)S(1)} collective-permute-done((bf16[80,1536]{1,0:T(8,128)(2,1)S(1)}, bf16[80,1536]{1,0:T(8,128)(2,1)S(1)}, u32[]{:S(2)}, u32[]{:S(2)}) %collective-permute-start.16) | collective-permute-done | bytes 245792 | tf_op jit(solution)/shard_map/ppermute | solution.py:33
  95.9 6.6 %shard_map.108 = (bf16[256,800]{1,0:T(8,128)(2,1)S(1)}, bf16[256,480]{1,0:T(8,128)(2,1)S(1)}, bf16[80,1536]{1,0:T(8,128)(2,1)S(1)}, bf16[80,1536]{1,0:T(8,128)(2...) custom-call(s32[1]{0:T(128)} %bitcast.core, ...), custom_call_target="tpu_custom_call" | custom-call | flops 4152360960 | bytes 15630336 | tf_op jit(solution)/shard_map/pallas_call | solution.py:218
  102.5 0.7 copy-done.9
  103.4 2.5 %shard_map.109 = (bf16[64,256]{1,0:T(8,128)(2,1)S(1)}, bf16[64,256]{1,0:T(8,128)(2,1)S(1)}) custom-call(bf16[256,800]{1,0:T(8,128)(2,1)S(1)} %get-tuple-element.37.first, bf16[256,480]{1,0:T(8,128)(2,1)S(1)} %get-tuple-element.38.second, bf16[1536,256]{1,0:T(8,128)(2,1)S(1)} %copy-done.2, bf16[1536,256]{1,0:T(8,128)(2,1)S(1)} %collective-permute-done.2.value_partner, ...), custom_call_target="tpu_custom_call" | custom-call | flops 1006632960 | bytes 4587520 | tf_op jit(solution)/shard_map/pallas_call | solution.py:268
  106.0 0.1 collective-permute-start.18
  106.1 3.3 %collective-permute-start.30 = (bf16[80,1536]{1,0:T(8,128)(2,1)}, bf16[80,1536]{1,0:T(8,128)(2,1)S(1)}, u32[]{:S(2)}, u32[]{:S(2)}) collective-permute-start(bf16[80,1536]{1,0:T(8,128)(2,1)} %copy-done.22), channel_id=1, source_target_pairs={{0,14},{1,15},{2,0},{3,1},{4,2},{5,3},{6,4},{7,5},{8,6},{9,7},{10,... | collective-permute-start | bytes 737288 | tf_op jit(solution)/shard_map/ppermute | solution.py:33
  109.4 0.1 collective-permute-start.20
  109.5 1.9 %collective-permute-start.23 = (bf16[80,1536]{1,0:T(8,128)(2,1)}, bf16[80,1536]{1,0:T(8,128)(2,1)S(1)}, u32[]{:S(2)}, u32[]{:S(2)}) collective-permute-start(bf16[80,1536]{1,0:T(8,128)(2,1)} %copy-done.20), channel_id=1, source_target_pairs={{0,2},{1,3},{2,4},{3,5},{4,6},{5,7},{6,8},{7,9},{8,10},{9,11},{10,... | collective-permute-start | bytes 737288 | tf_op jit(solution)/shard_map/ppermute | solution.py:33
  111.5 2.2 %copy-done.1 = bf16[256,8192]{1,0:T(8,128)(2,1)S(1)} copy-done((bf16[256,8192]{1,0:T(8,128)(2,1)S(1)}, bf16[256,8192]{1,0:T(8,128)(2,1)}, u32[]{:S(2)}) %copy-start.1) | copy-done | bytes 4194328
  113.7 2.3 %shard_map.110 = (f32[8,128,512]{2,1,0:T(8,128)S(1)}, f32[8,128,512]{2,1,0:T(8,128)S(1)}) custom-call(s32[1]{0:T(128)} %bitcast.core, bf16[128,256]{1,0:T(8,128)(2,1)S(1)} %maximum_select_fusion.attended, bf16[256,8192]{1,0:T(8,128)(2,1)S(1)} %copy-done.1), custom_call_target="tpu_custom_call" | custom-call | flops 536870912 | bytes 12582912 | tf_op jit(solution)/shard_map/pallas_call | solution.py:71
  116.0 0.3 collective-permute-start.19
  116.3 1.0 add_convert_fusion.6
  117.5 3.3 %collective-permute-start.31 = (bf16[80,1536]{1,0:T(8,128)(2,1)S(1)}, bf16[80,1536]{1,0:T(8,128)(2,1)S(1)}, u32[]{:S(2)}, u32[]{:S(2)}) collective-permute-start(bf16[80,1536]{1,0:T(8,128)(2,1)S(1)} %add_convert_fusion.4), channel_id=1, source_target_pairs={{0,14},{1,15},{2,0},{3,1},{4,2},{5,3},{6,4},{7,5},{8,6},{9,7},{10,... | collective-permute-start | bytes 737288 | tf_op jit(solution)/shard_map/ppermute | solution.py:33
  120.9 3.7 %collective-permute-start.21 = (bf16[80,1536]{1,0:T(8,128)(2,1)S(1)}, bf16[80,1536]{1,0:T(8,128)(2,1)S(1)}, u32[]{:S(2)}, u32[]{:S(2)}) collective-permute-start(bf16[80,1536]{1,0:T(8,128)(2,1)S(1)} %add_convert_fusion.12), channel_id=1, source_target_pairs={{0,14},{1,15},{2,0},{3,1},{4,2},{5,3},{6,4},{7,5},{8,6},{9,7},{10,... | collective-permute-start | bytes 737288 | tf_op jit(solution)/shard_map/ppermute | solution.py:33
  124.5 1.0 add_convert_fusion.10
  125.6 1.3 collective-permute-done.28
  127.2 3.7 %collective-permute-start.32 = (bf16[80,1536]{1,0:T(8,128)(2,1)S(1)}, bf16[80,1536]{1,0:T(8,128)(2,1)S(1)}, u32[]{:S(2)}, u32[]{:S(2)}) collective-permute-start(bf16[80,1536]{1,0:T(8,128)(2,1)S(1)} %add_convert_fusion.3), channel_id=1, source_target_pairs={{0,14},{1,15},{2,0},{3,1},{4,2},{5,3},{6,4},{7,5},{8,6},{9,7},{10,... | collective-permute-start | bytes 737288 | tf_op jit(solution)/shard_map/ppermute | solution.py:33
  130.9 1.4 collective-permute-done.21
  132.4 3.8 %collective-permute-start.22 = (bf16[80,1536]{1,0:T(8,128)(2,1)S(1)}, bf16[80,1536]{1,0:T(8,128)(2,1)S(1)}, u32[]{:S(2)}, u32[]{:S(2)}) collective-permute-start(bf16[80,1536]{1,0:T(8,128)(2,1)S(1)} %add_convert_fusion.11), channel_id=1, source_target_pairs={{0,14},{1,15},{2,0},{3,1},{4,2},{5,3},{6,4},{7,5},{8,6},{9,7},{10,... | collective-permute-start | bytes 737288 | tf_op jit(solution)/shard_map/ppermute | solution.py:33
  136.4 1.3 collective-permute-done.32
  137.7 3.8 %collective-permute-start.33 = (bf16[80,1536]{1,0:T(8,128)(2,1)S(1)}, bf16[80,1536]{1,0:T(8,128)(2,1)S(1)}, u32[]{:S(2)}, u32[]{:S(2)}) collective-permute-start(bf16[80,1536]{1,0:T(8,128)(2,1)S(1)} %add_convert_fusion.2), channel_id=1, source_target_pairs={{0,14},{1,15},{2,0},{3,1},{4,2},{5,3},{6,4},{7,5},{8,6},{9,7},{10,... | collective-permute-start | bytes 737288 | tf_op jit(solution)/shard_map/ppermute | solution.py:33
  141.5 1.4 add_convert_fusion
  142.9 1.7 collective-permute-done.25
  144.7 2.7 %collective-permute-done.33 = bf16[80,1536]{1,0:T(8,128)(2,1)S(1)} collective-permute-done((bf16[80,1536]{1,0:T(8,128)(2,1)S(1)}, bf16[80,1536]{1,0:T(8,128)(2,1)S(1)}, u32[]{:S(2)}, u32[]{:S(2)}) %collective-permute-start.33) | collective-permute-done | bytes 245792 | tf_op jit(solution)/shard_map/ppermute | solution.py:33
  147.4 0.1 add_convert_fusion.1
  147.5 0.1 collective-permute-start.34
  147.6 4.5 %collective-permute-done.26 = bf16[80,1536]{1,0:T(8,128)(2,1)S(1)} collective-permute-done((bf16[80,1536]{1,0:T(8,128)(2,1)S(1)}, bf16[80,1536]{1,0:T(8,128)(2,1)S(1)}, u32[]{:S(2)}, u32[]{:S(2)}) %collective-permute-start.26) | collective-permute-done | bytes 245792 | tf_op jit(solution)/shard_map/ppermute | solution.py:33
  152.1 0.8 fusion.10.first
  152.9 0.7 copy-done.25
  153.6 2.7 %shard_map.111 = bf16[32,8,1536]{2,1,0:T(8,128)(2,1)} custom-call(s32[1]{0:T(128)} %bitcast.core, s32[32]{0:T(128)} %copy-done.26, bf16[10,8,1536]{2,1,0:T(8,128)(2,1)} %fusion.10.first, bf16[10,8,1536]{2,1,0:T(8,128)(2,1)} %bitcast.22), custom_call_target="tpu_custom_call" | custom-call | bytes 1572864 | tf_op jit(solution)/shard_map/pallas_call | solution.py:306
  156.3 17.4 %all_to_all.10 = bf16[16,2,8,1536]{3,2,1,0:T(8,128)(2,1)} all-to-all(bf16[16,2,8,1536]{3,2,1,0:T(8,128)(2,1)} %bitcast.19), channel_id=1, replica_groups=mesh['dp'=16,'mp'=16] {'dp'}, dimensions={0} | all-to-all | bytes 1572864 | tf_op jit(solution)/shard_map/all_to_all | solution.py:482
  173.7 2.3 %shard_map.112 = bf16[32,8,1536]{2,1,0:T(8,128)(2,1)} custom-call(s32[32]{0:T(128)} %get-tuple-element.43.source, bf16[32,8,1536]{2,1,0:T(8,128)(2,1)} %bitcast.20), custom_call_target="tpu_custom_call" | custom-call | bytes 1572864 | tf_op jit(solution)/shard_map/pallas_call | solution.py:319
  176.1 3.5 %reduce-scatter.2.cloned.1.call-done = bf16[1,128,512]{2,1,0:T(8,128)(2,1)} async-done(((bf16[8,128,512]{2,1,0:T(8,128)(2,1)}), bf16[1,128,512]{2,1,0:T(8,128)(2,1)}) %reduce-scatter.2.cloned.1.call-update) | async-done | bytes 131088 | tf_op jit(solution)/shard_map/reduce_scatter | solution.py:475
  (100 shorter events, 1.4 us)
Async XLA Ops:
  7.2 55.8 %all-gather.2.cloned.1.call-start = ((), (), s32[]{:S(2)}) async-start(), calls=%async_computation.3 | async-start | bytes 4456448 | tf_op jit(solution)/shard_map/all_gather | solution.py:392
  10.1 20.2 %all-to-all-start = ((bf16[16,2,8,1664]{3,2,1,0:T(8,128)(2,1)}), bf16[16,2,8,1664]{3,2,1,0:T(8,128)(2,1)S(1)}, u32[]{:S(2)}, u32[]{:S(2)}) async-start(bf16[16,2,8,1664]{3,2,1,0:T(8,128)(2,1)} %bitcast.21), calls=%async_computation | async-start | bytes 1703936 | tf_op jit(solution)/shard_map/all_to_all | solution.py:393
  17.6 161.9 %reduce-scatter.2.cloned.1.call-start = ((), (), s32[]{:S(2)}) async-start(), calls=%async_computation.4 | async-start | bytes 1179648 | tf_op jit(solution)/shard_map/reduce_scatter | solution.py:475
  17.7 25.4 %collective-permute-start.2 = (bf16[1536,256]{1,0:T(8,128)(2,1)}, bf16[1536,256]{1,0:T(8,128)(2,1)S(1)}, u32[]{:S(2)}, u32[]{:S(2)}) collective-permute-start(bf16[1536,256]{1,0:T(8,128)(2,1)} %value_own.3), channel_id=1, source_target_pairs={{0,1},{1,0},{2,3},{3,2},{4,5},{5,4},{6,7},{7,6},{8,9},{9,8},{10,11... | collective-permute-start | bytes 2359304 | tf_op jit(solution)/shard_map/ppermute | solution.py:37
  30.3 2.0 %copy-start.24 = (bf16[16,2,8,1664]{3,2,1,0:T(8,128)(2,1)}, bf16[16,2,8,1664]{3,2,1,0:T(8,128)(2,1)S(1)}, u32[]{:S(2)}) copy-start(bf16[16,2,8,1664]{3,2,1,0:T(8,128)(2,1)S(1)} %all-to-all-done) | copy-start | bytes 2555908
  34.5 1.9 %collective-permute-start.3 = (bf16[80,1536]{1,0:T(8,128)(2,1)}, bf16[80,1536]{1,0:T(8,128)(2,1)S(1)}, u32[]{:S(2)}, u32[]{:S(2)}) collective-permute-start(bf16[80,1536]{1,0:T(8,128)(2,1)} %bitcast.23), channel_id=1, source_target_pairs={{0,1},{1,0},{2,3},{3,2},{4,5},{5,4},{6,7},{7,6},{8,9},{9,8},{10,11... | collective-permute-start | bytes 737288 | tf_op jit(solution)/shard_map/ppermute | solution.py:37
  34.5 17.7 %collective-permute-start.4 = (bf16[80,1536]{1,0:T(8,128)(2,1)}, bf16[80,1536]{1,0:T(8,128)(2,1)S(1)}, u32[]{:S(2)}, u32[]{:S(2)}) collective-permute-start(bf16[80,1536]{1,0:T(8,128)(2,1)} %bitcast.13), channel_id=1, source_target_pairs={{0,2},{1,3},{2,4},{3,5},{4,6},{5,7},{6,8},{7,9},{8,10},{9,11},{10,... | collective-permute-start | bytes 737288 | tf_op jit(solution)/shard_map/ppermute | solution.py:33
  36.4 17.0 %collective-permute-start.7 = (bf16[80,1536]{1,0:T(8,128)(2,1)S(1)}, bf16[80,1536]{1,0:T(8,128)(2,1)S(1)}, u32[]{:S(2)}, u32[]{:S(2)}) collective-permute-start(bf16[80,1536]{1,0:T(8,128)(2,1)S(1)} %collective-permute-done.3.refs_1_), channel_id=1, source_target_pairs={{0,14},{1,15},{2,0},{3,1},{4,2},{5,3},{6,4},{7,5},{8,6},{9,7},{10,... | collective-permute-start | bytes 737288 | tf_op jit(solution)/shard_map/ppermute | solution.py:33
  42.0 33.2 %collective-permute-start.1 = (bf16[1536,256]{1,0:T(8,128)(2,1)}, bf16[1536,256]{1,0:T(8,128)(2,1)S(1)}, u32[]{:S(2)}, u32[]{:S(2)}) collective-permute-start(bf16[1536,256]{1,0:T(8,128)(2,1)} %key_own.1), channel_id=1, source_target_pairs={{0,1},{1,0},{2,3},{3,2},{4,5},{5,4},{6,7},{7,6},{8,9},{9,8},{10,11... | collective-permute-start | bytes 2359304 | tf_op jit(solution)/shard_map/ppermute | solution.py:37
  42.0 24.6 %collective-permute-start.6 = (bf16[80,1536]{1,0:T(8,128)(2,1)}, bf16[80,1536]{1,0:T(8,128)(2,1)S(1)}, u32[]{:S(2)}, u32[]{:S(2)}) collective-permute-start(bf16[80,1536]{1,0:T(8,128)(2,1)} %bitcast.14), channel_id=1, source_target_pairs={{0,14},{1,15},{2,0},{3,1},{4,2},{5,3},{6,4},{7,5},{8,6},{9,7},{10,... | collective-permute-start | bytes 737288 | tf_op jit(solution)/shard_map/ppermute | solution.py:33
  43.1 25.7 %collective-permute-start.5 = (bf16[80,1536]{1,0:T(8,128)(2,1)S(1)}, bf16[80,1536]{1,0:T(8,128)(2,1)S(1)}, u32[]{:S(2)}, u32[]{:S(2)}) collective-permute-start(bf16[80,1536]{1,0:T(8,128)(2,1)S(1)} %collective-permute-done.3.refs_1_), channel_id=1, source_target_pairs={{0,2},{1,3},{2,4},{3,5},{4,6},{5,7},{6,8},{7,9},{8,10},{9,11},{10,... | collective-permute-start | bytes 737288 | tf_op jit(solution)/shard_map/ppermute | solution.py:33
  52.1 16.0 %collective-permute-start.8 = (bf16[80,1536]{1,0:T(8,128)(2,1)S(1)}, bf16[80,1536]{1,0:T(8,128)(2,1)S(1)}, u32[]{:S(2)}, u32[]{:S(2)}) collective-permute-start(bf16[80,1536]{1,0:T(8,128)(2,1)S(1)} %collective-permute-done.4.refs_2_), channel_id=1, source_target_pairs={{0,2},{1,3},{2,4},{3,5},{4,6},{5,7},{6,8},{7,9},{8,10},{9,11},{10,... | collective-permute-start | bytes 737288 | tf_op jit(solution)/shard_map/ppermute | solution.py:33
  53.4 16.0 %collective-permute-start.11 = (bf16[80,1536]{1,0:T(8,128)(2,1)S(1)}, bf16[80,1536]{1,0:T(8,128)(2,1)S(1)}, u32[]{:S(2)}, u32[]{:S(2)}) collective-permute-start(bf16[80,1536]{1,0:T(8,128)(2,1)S(1)} %collective-permute-done.7.refs_5_), channel_id=1, source_target_pairs={{0,14},{1,15},{2,0},{3,1},{4,2},{5,3},{6,4},{7,5},{8,6},{9,7},{10,... | collective-permute-start | bytes 737288 | tf_op jit(solution)/shard_map/ppermute | solution.py:33
  63.0 9.1 %copy-start = (bf16[256,8192]{1,0:T(8,128)(2,1)S(1)}, bf16[256,8192]{1,0:T(8,128)(2,1)}, u32[]{:S(2)}) copy-start(bf16[256,8192]{1,0:T(8,128)(2,1)} %w_out.1) | copy-start | bytes 12582916
  66.6 15.8 %copy-start.2 = (bf16[1536,256]{1,0:T(8,128)(2,1)S(1)}, bf16[1536,256]{1,0:T(8,128)(2,1)}, u32[]{:S(2)}) copy-start(bf16[1536,256]{1,0:T(8,128)(2,1)} %value_own.3) | copy-start | bytes 2359300
  66.7 15.8 %copy-start.4 = (bf16[1536,256]{1,0:T(8,128)(2,1)S(1)}, bf16[1536,256]{1,0:T(8,128)(2,1)}, u32[]{:S(2)}) copy-start(bf16[1536,256]{1,0:T(8,128)(2,1)} %key_own.1) | copy-start | bytes 2359300
  66.7 8.9 %collective-permute-start.10 = (bf16[80,1536]{1,0:T(8,128)(2,1)S(1)}, bf16[80,1536]{1,0:T(8,128)(2,1)S(1)}, u32[]{:S(2)}, u32[]{:S(2)}) collective-permute-start(bf16[80,1536]{1,0:T(8,128)(2,1)S(1)} %collective-permute-done.6.refs_4_), channel_id=1, source_target_pairs={{0,14},{1,15},{2,0},{3,1},{4,2},{5,3},{6,4},{7,5},{8,6},{9,7},{10,... | collective-permute-start | bytes 737288 | tf_op jit(solution)/shard_map/ppermute | solution.py:33
  68.2 15.5 %collective-permute-start.12 = (bf16[80,1536]{1,0:T(8,128)(2,1)S(1)}, bf16[80,1536]{1,0:T(8,128)(2,1)S(1)}, u32[]{:S(2)}, u32[]{:S(2)}) collective-permute-start(bf16[80,1536]{1,0:T(8,128)(2,1)S(1)} %collective-permute-done.8.refs_6_), channel_id=1, source_target_pairs={{0,2},{1,3},{2,4},{3,5},{4,6},{5,7},{6,8},{7,9},{8,10},{9,11},{10,... | collective-permute-start | bytes 737288 | tf_op jit(solution)/shard_map/ppermute | solution.py:33
  68.8 13.7 %collective-permute-start.9 = (bf16[80,1536]{1,0:T(8,128)(2,1)S(1)}, bf16[80,1536]{1,0:T(8,128)(2,1)S(1)}, u32[]{:S(2)}, u32[]{:S(2)}) collective-permute-start(bf16[80,1536]{1,0:T(8,128)(2,1)S(1)} %collective-permute-done.5.refs_3_), channel_id=1, source_target_pairs={{0,2},{1,3},{2,4},{3,5},{4,6},{5,7},{6,8},{7,9},{8,10},{9,11},{10,... | collective-permute-start | bytes 737288 | tf_op jit(solution)/shard_map/ppermute | solution.py:33
  69.4 14.3 %collective-permute-start.15 = (bf16[80,1536]{1,0:T(8,128)(2,1)S(1)}, bf16[80,1536]{1,0:T(8,128)(2,1)S(1)}, u32[]{:S(2)}, u32[]{:S(2)}) collective-permute-start(bf16[80,1536]{1,0:T(8,128)(2,1)S(1)} %collective-permute-done.11.refs_9_), channel_id=1, source_target_pairs={{0,14},{1,15},{2,0},{3,1},{4,2},{5,3},{6,4},{7,5},{8,6},{9,7},{10,... | collective-permute-start | bytes 737288 | tf_op jit(solution)/shard_map/ppermute | solution.py:33
  75.2 11.9 %copy-start.3 = (bf16[10,8,1536]{2,1,0:T(8,128)(2,1)S(1)}, bf16[10,8,1536]{2,1,0:T(8,128)(2,1)}, u32[]{:S(2)}) copy-start(bf16[10,8,1536]{2,1,0:T(8,128)(2,1)} %get-tuple-element.33) | copy-start | bytes 737284
  75.2 7.2 %collective-permute-start = (bf16[64,512]{1,0:T(8,128)(2,1)S(1)}, bf16[64,512]{1,0:T(8,128)(2,1)S(1)}, u32[]{:S(2)}, u32[]{:S(2)}) collective-permute-start(bf16[64,512]{1,0:T(8,128)(2,1)S(1)} %get-tuple-element.60), channel_id=1, source_target_pairs={{0,1},{1,0},{2,3},{3,2},{4,5},{5,4},{6,7},{7,6},{8,9},{9,8},{10,11... | collective-permute-start | bytes 196616 | tf_op jit(solution)/shard_map/ppermute | solution.py:37
  75.5 14.7 %collective-permute-start.14 = (bf16[80,1536]{1,0:T(8,128)(2,1)S(1)}, bf16[80,1536]{1,0:T(8,128)(2,1)S(1)}, u32[]{:S(2)}, u32[]{:S(2)}) collective-permute-start(bf16[80,1536]{1,0:T(8,128)(2,1)S(1)} %collective-permute-done.10.refs_8_), channel_id=1, source_target_pairs={{0,14},{1,15},{2,0},{3,1},{4,2},{5,3},{6,4},{7,5},{8,6},{9,7},{10,... | collective-permute-start | bytes 737288 | tf_op jit(solution)/shard_map/ppermute | solution.py:33
  82.5 10.1 %collective-permute-start.13 = (bf16[80,1536]{1,0:T(8,128)(2,1)S(1)}, bf16[80,1536]{1,0:T(8,128)(2,1)S(1)}, u32[]{:S(2)}, u32[]{:S(2)}) collective-permute-start(bf16[80,1536]{1,0:T(8,128)(2,1)S(1)} %collective-permute-done.9.refs_7_), channel_id=1, source_target_pairs={{0,2},{1,3},{2,4},{3,5},{4,6},{5,7},{6,8},{7,9},{8,10},{9,11},{10,... | collective-permute-start | bytes 737288 | tf_op jit(solution)/shard_map/ppermute | solution.py:33
  83.7 12.2 %copy-start.23 = (s32[2]{0:T(128)S(1)}, s32[2]{0:T(128)}, u32[]{:S(2)}) copy-start(s32[2]{0:T(128)} %counts.1) | copy-start | bytes 28
  83.7 12.2 %collective-permute-start.16 = (bf16[80,1536]{1,0:T(8,128)(2,1)S(1)}, bf16[80,1536]{1,0:T(8,128)(2,1)S(1)}, u32[]{:S(2)}, u32[]{:S(2)}) collective-permute-start(bf16[80,1536]{1,0:T(8,128)(2,1)S(1)} %collective-permute-done.12.refs_0_.refs_10_), channel_id=1, source_target_pairs={{0,2},{1,3},{2,4},{3,5},{4,6},{5,7},{6,8},{7,9},{8,10},{9,11},{10,... | collective-permute-start | bytes 737288 | tf_op jit(solution)/shard_map/ppermute | solution.py:33
  83.8 12.1 %collective-permute-start.17 = (bf16[80,1536]{1,0:T(8,128)(2,1)S(1)}, bf16[80,1536]{1,0:T(8,128)(2,1)S(1)}, u32[]{:S(2)}, u32[]{:S(2)}) collective-permute-start(bf16[80,1536]{1,0:T(8,128)(2,1)S(1)} %collective-permute-done.15.refs_3_.refs_13_), channel_id=1, source_target_pairs={{0,14},{1,15},{2,0},{3,1},{4,2},{5,3},{6,4},{7,5},{8,6},{9,7},{10,... | collective-permute-start | bytes 737288 | tf_op jit(solution)/shard_map/ppermute | solution.py:33
  102.5 0.7 copy-start.9
  103.2 2.7 %copy-start.5 = (bf16[80,1536]{1,0:T(8,128)(2,1)}, bf16[80,1536]{1,0:T(8,128)(2,1)S(1)}, u32[]{:S(2)}) copy-start(bf16[80,1536]{1,0:T(8,128)(2,1)S(1)} %get-tuple-element.58) | copy-start | bytes 737284
  103.2 2.7 %copy-start.7 = (bf16[80,1536]{1,0:T(8,128)(2,1)}, bf16[80,1536]{1,0:T(8,128)(2,1)S(1)}, u32[]{:S(2)}) copy-start(bf16[80,1536]{1,0:T(8,128)(2,1)S(1)} %get-tuple-element.55) | copy-start | bytes 737284
  103.2 2.7 %copy-start.10 = (bf16[80,1536]{1,0:T(8,128)(2,1)}, bf16[80,1536]{1,0:T(8,128)(2,1)S(1)}, u32[]{:S(2)}) copy-start(bf16[80,1536]{1,0:T(8,128)(2,1)S(1)} %get-tuple-element.46) | copy-start | bytes 737284
  103.2 2.7 %copy-start.12 = (bf16[80,1536]{1,0:T(8,128)(2,1)}, bf16[80,1536]{1,0:T(8,128)(2,1)S(1)}, u32[]{:S(2)}) copy-start(bf16[80,1536]{1,0:T(8,128)(2,1)S(1)} %get-tuple-element.57) | copy-start | bytes 737284
  103.2 2.7 %copy-start.14 = (bf16[80,1536]{1,0:T(8,128)(2,1)}, bf16[80,1536]{1,0:T(8,128)(2,1)S(1)}, u32[]{:S(2)}) copy-start(bf16[80,1536]{1,0:T(8,128)(2,1)S(1)} %get-tuple-element.54) | copy-start | bytes 737284
  103.2 2.7 %copy-start.16 = (bf16[80,1536]{1,0:T(8,128)(2,1)}, bf16[80,1536]{1,0:T(8,128)(2,1)S(1)}, u32[]{:S(2)}) copy-start(bf16[80,1536]{1,0:T(8,128)(2,1)S(1)} %get-tuple-element.44) | copy-start | bytes 737284
  103.2 2.7 %copy-start.18 = (bf16[80,1536]{1,0:T(8,128)(2,1)}, bf16[80,1536]{1,0:T(8,128)(2,1)S(1)}, u32[]{:S(2)}) copy-start(bf16[80,1536]{1,0:T(8,128)(2,1)S(1)} %get-tuple-element.52) | copy-start | bytes 737284
  103.2 2.7 %copy-start.20 = (bf16[80,1536]{1,0:T(8,128)(2,1)}, bf16[80,1536]{1,0:T(8,128)(2,1)S(1)}, u32[]{:S(2)}) copy-start(bf16[80,1536]{1,0:T(8,128)(2,1)S(1)} %get-tuple-element.48) | copy-start | bytes 737284
  103.3 2.7 %copy-start.21 = (bf16[80,1536]{1,0:T(8,128)(2,1)}, bf16[80,1536]{1,0:T(8,128)(2,1)S(1)}, u32[]{:S(2)}) copy-start(bf16[80,1536]{1,0:T(8,128)(2,1)S(1)} %get-tuple-element.45) | copy-start | bytes 737284
  103.3 2.7 %copy-start.22 = (bf16[80,1536]{1,0:T(8,128)(2,1)}, bf16[80,1536]{1,0:T(8,128)(2,1)S(1)}, u32[]{:S(2)}) copy-start(bf16[80,1536]{1,0:T(8,128)(2,1)S(1)} %get-tuple-element.56) | copy-start | bytes 737284
  103.3 13.0 %collective-permute-start.27 = (bf16[80,1536]{1,0:T(8,128)(2,1)}, bf16[80,1536]{1,0:T(8,128)(2,1)}, u32[]{:S(2)}, u32[]{:S(2)}) collective-permute-start(bf16[80,1536]{1,0:T(8,128)(2,1)} %get-tuple-element.53), channel_id=1, source_target_pairs={{0,2},{1,3},{2,4},{3,5},{4,6},{5,7},{6,8},{7,9},{8,10},{9,11},{10,... | collective-permute-start | bytes 737288 | tf_op jit(solution)/shard_map/ppermute | solution.py:33
  106.0 5.4 %collective-permute-start.18 = (bf16[64,256]{1,0:T(8,128)(2,1)S(1)}, bf16[64,256]{1,0:T(8,128)(2,1)S(1)}, u32[]{:S(2)}, u32[]{:S(2)}) collective-permute-start(bf16[64,256]{1,0:T(8,128)(2,1)S(1)} %get-tuple-element.40), channel_id=1, source_target_pairs={{0,1},{1,0},{2,3},{3,2},{4,5},{5,4},{6,7},{7,6},{8,9},{9,8},{10,11... | collective-permute-start | bytes 98312 | tf_op jit(solution)/shard_map/ppermute | solution.py:37
  106.1 11.3 %collective-permute-start.30 = (bf16[80,1536]{1,0:T(8,128)(2,1)}, bf16[80,1536]{1,0:T(8,128)(2,1)S(1)}, u32[]{:S(2)}, u32[]{:S(2)}) collective-permute-start(bf16[80,1536]{1,0:T(8,128)(2,1)} %copy-done.22), channel_id=1, source_target_pairs={{0,14},{1,15},{2,0},{3,1},{4,2},{5,3},{6,4},{7,5},{8,6},{9,7},{10,... | collective-permute-start | bytes 737288 | tf_op jit(solution)/shard_map/ppermute | solution.py:33
  109.4 11.4 %collective-permute-start.20 = (bf16[80,1536]{1,0:T(8,128)(2,1)}, bf16[80,1536]{1,0:T(8,128)(2,1)S(1)}, u32[]{:S(2)}, u32[]{:S(2)}) collective-permute-start(bf16[80,1536]{1,0:T(8,128)(2,1)} %copy-done.21), channel_id=1, source_target_pairs={{0,14},{1,15},{2,0},{3,1},{4,2},{5,3},{6,4},{7,5},{8,6},{9,7},{10,... | collective-permute-start | bytes 737288 | tf_op jit(solution)/shard_map/ppermute | solution.py:33
  109.5 15.0 %collective-permute-start.23 = (bf16[80,1536]{1,0:T(8,128)(2,1)}, bf16[80,1536]{1,0:T(8,128)(2,1)S(1)}, u32[]{:S(2)}, u32[]{:S(2)}) collective-permute-start(bf16[80,1536]{1,0:T(8,128)(2,1)} %copy-done.20), channel_id=1, source_target_pairs={{0,2},{1,3},{2,4},{3,5},{4,6},{5,7},{6,8},{7,9},{8,10},{9,11},{10,... | collective-permute-start | bytes 737288 | tf_op jit(solution)/shard_map/ppermute | solution.py:33
  111.5 2.2 %copy-start.1 = (bf16[256,8192]{1,0:T(8,128)(2,1)S(1)}, bf16[256,8192]{1,0:T(8,128)(2,1)}, u32[]{:S(2)}) copy-start(bf16[256,8192]{1,0:T(8,128)(2,1)} %w_out.1) | copy-start | bytes 12582916
  113.6 2.7 %copy-start.15 = (bf16[80,1536]{1,0:T(8,128)(2,1)S(1)}, bf16[80,1536]{1,0:T(8,128)(2,1)}, u32[]{:S(2)}) copy-start(bf16[80,1536]{1,0:T(8,128)(2,1)} %copy-done.14) | copy-start | bytes 737284
  113.7 3.8 %copy-start.13 = (bf16[80,1536]{1,0:T(8,128)(2,1)S(1)}, bf16[80,1536]{1,0:T(8,128)(2,1)}, u32[]{:S(2)}) copy-start(bf16[80,1536]{1,0:T(8,128)(2,1)} %copy-done.12) | copy-start | bytes 737284
  113.7 7.2 %copy-start.11 = (bf16[80,1536]{1,0:T(8,128)(2,1)S(1)}, bf16[80,1536]{1,0:T(8,128)(2,1)}, u32[]{:S(2)}) copy-start(bf16[80,1536]{1,0:T(8,128)(2,1)} %copy-done.10) | copy-start | bytes 737284
  113.7 13.3 %copy-start.8 = (bf16[80,1536]{1,0:T(8,128)(2,1)S(1)}, bf16[80,1536]{1,0:T(8,128)(2,1)}, u32[]{:S(2)}) copy-start(bf16[80,1536]{1,0:T(8,128)(2,1)} %copy-done.7) | copy-start | bytes 737284
  113.7 13.5 %copy-start.6 = (bf16[80,1536]{1,0:T(8,128)(2,1)S(1)}, bf16[80,1536]{1,0:T(8,128)(2,1)}, u32[]{:S(2)}) copy-start(bf16[80,1536]{1,0:T(8,128)(2,1)} %copy-done.5) | copy-start | bytes 737284
  116.0 25.5 %collective-permute-start.19 = (f32[8,128,512]{2,1,0:T(8,128)S(1)}, f32[8,128,512]{2,1,0:T(8,128)S(1)}, u32[]{:S(2)}, u32[]{:S(2)}) collective-permute-start(f32[8,128,512]{2,1,0:T(8,128)S(1)} %get-tuple-element.42), channel_id=1, source_target_pairs={{0,1},{1,0},{2,3},{3,2},{4,5},{5,4},{6,7},{7,6},{8,9},{9,8},{10,11... | collective-permute-start | bytes 6291464 | tf_op jit(solution)/shard_map/ppermute | solution.py:37
  117.3 9.6 %collective-permute-start.28 = (bf16[80,1536]{1,0:T(8,128)(2,1)S(1)}, bf16[80,1536]{1,0:T(8,128)(2,1)S(1)}, u32[]{:S(2)}, u32[]{:S(2)}) collective-permute-start(bf16[80,1536]{1,0:T(8,128)(2,1)S(1)} %add_convert_fusion.6), channel_id=1, source_target_pairs={{0,2},{1,3},{2,4},{3,5},{4,6},{5,7},{6,8},{7,9},{8,10},{9,11},{10,... | collective-permute-start | bytes 737288 | tf_op jit(solution)/shard_map/ppermute | solution.py:33
  117.5 9.6 %collective-permute-start.31 = (bf16[80,1536]{1,0:T(8,128)(2,1)S(1)}, bf16[80,1536]{1,0:T(8,128)(2,1)S(1)}, u32[]{:S(2)}, u32[]{:S(2)}) collective-permute-start(bf16[80,1536]{1,0:T(8,128)(2,1)S(1)} %add_convert_fusion.4), channel_id=1, source_target_pairs={{0,14},{1,15},{2,0},{3,1},{4,2},{5,3},{6,4},{7,5},{8,6},{9,7},{10,... | collective-permute-start | bytes 737288 | tf_op jit(solution)/shard_map/ppermute | solution.py:33
  120.9 11.5 %collective-permute-start.21 = (bf16[80,1536]{1,0:T(8,128)(2,1)S(1)}, bf16[80,1536]{1,0:T(8,128)(2,1)S(1)}, u32[]{:S(2)}, u32[]{:S(2)}) collective-permute-start(bf16[80,1536]{1,0:T(8,128)(2,1)S(1)} %add_convert_fusion.12), channel_id=1, source_target_pairs={{0,14},{1,15},{2,0},{3,1},{4,2},{5,3},{6,4},{7,5},{8,6},{9,7},{10,... | collective-permute-start | bytes 737288 | tf_op jit(solution)/shard_map/ppermute | solution.py:33
  125.5 10.7 %collective-permute-start.24 = (bf16[80,1536]{1,0:T(8,128)(2,1)S(1)}, bf16[80,1536]{1,0:T(8,128)(2,1)S(1)}, u32[]{:S(2)}, u32[]{:S(2)}) collective-permute-start(bf16[80,1536]{1,0:T(8,128)(2,1)S(1)} %add_convert_fusion.10), channel_id=1, source_target_pairs={{0,2},{1,3},{2,4},{3,5},{4,6},{5,7},{6,8},{7,9},{8,10},{9,11},{10,... | collective-permute-start | bytes 737288 | tf_op jit(solution)/shard_map/ppermute | solution.py:33
  127.0 17.7 %collective-permute-start.29 = (bf16[80,1536]{1,0:T(8,128)(2,1)S(1)}, bf16[80,1536]{1,0:T(8,128)(2,1)S(1)}, u32[]{:S(2)}, u32[]{:S(2)}) collective-permute-start(bf16[80,1536]{1,0:T(8,128)(2,1)S(1)} %add_convert_fusion.5), channel_id=1, source_target_pairs={{0,2},{1,3},{2,4},{3,5},{4,6},{5,7},{6,8},{7,9},{8,10},{9,11},{10,... | collective-permute-start | bytes 737288 | tf_op jit(solution)/shard_map/ppermute | solution.py:33
  127.2 10.4 %collective-permute-start.32 = (bf16[80,1536]{1,0:T(8,128)(2,1)S(1)}, bf16[80,1536]{1,0:T(8,128)(2,1)S(1)}, u32[]{:S(2)}, u32[]{:S(2)}) collective-permute-start(bf16[80,1536]{1,0:T(8,128)(2,1)S(1)} %add_convert_fusion.3), channel_id=1, source_target_pairs={{0,14},{1,15},{2,0},{3,1},{4,2},{5,3},{6,4},{7,5},{8,6},{9,7},{10,... | collective-permute-start | bytes 737288 | tf_op jit(solution)/shard_map/ppermute | solution.py:33
  132.4 15.2 %collective-permute-start.22 = (bf16[80,1536]{1,0:T(8,128)(2,1)S(1)}, bf16[80,1536]{1,0:T(8,128)(2,1)S(1)}, u32[]{:S(2)}, u32[]{:S(2)}) collective-permute-start(bf16[80,1536]{1,0:T(8,128)(2,1)S(1)} %add_convert_fusion.11), channel_id=1, source_target_pairs={{0,14},{1,15},{2,0},{3,1},{4,2},{5,3},{6,4},{7,5},{8,6},{9,7},{10,... | collective-permute-start | bytes 737288 | tf_op jit(solution)/shard_map/ppermute | solution.py:33
  136.2 11.2 %copy-start.19 = (bf16[80,1536]{1,0:T(8,128)(2,1)S(1)}, bf16[80,1536]{1,0:T(8,128)(2,1)}, u32[]{:S(2)}) copy-start(bf16[80,1536]{1,0:T(8,128)(2,1)} %copy-done.18) | copy-start | bytes 737284
  136.3 8.3 %collective-permute-start.25 = (bf16[80,1536]{1,0:T(8,128)(2,1)S(1)}, bf16[80,1536]{1,0:T(8,128)(2,1)S(1)}, u32[]{:S(2)}, u32[]{:S(2)}) collective-permute-start(bf16[80,1536]{1,0:T(8,128)(2,1)S(1)} %add_convert_fusion.9), channel_id=1, source_target_pairs={{0,2},{1,3},{2,4},{3,5},{4,6},{5,7},{6,8},{7,9},{8,10},{9,11},{10,... | collective-permute-start | bytes 737288 | tf_op jit(solution)/shard_map/ppermute | solution.py:33
  137.7 14.4 %copy-start.17 = (bf16[80,1536]{1,0:T(8,128)(2,1)S(1)}, bf16[80,1536]{1,0:T(8,128)(2,1)}, u32[]{:S(2)}) copy-start(bf16[80,1536]{1,0:T(8,128)(2,1)} %copy-done.16) | copy-start | bytes 737284
  137.7 9.7 %collective-permute-start.33 = (bf16[80,1536]{1,0:T(8,128)(2,1)S(1)}, bf16[80,1536]{1,0:T(8,128)(2,1)S(1)}, u32[]{:S(2)}, u32[]{:S(2)}) collective-permute-start(bf16[80,1536]{1,0:T(8,128)(2,1)S(1)} %add_convert_fusion.2), channel_id=1, source_target_pairs={{0,14},{1,15},{2,0},{3,1},{4,2},{5,3},{6,4},{7,5},{8,6},{9,7},{10,... | collective-permute-start | bytes 737288 | tf_op jit(solution)/shard_map/ppermute | solution.py:33
  144.6 7.5 %collective-permute-start.26 = (bf16[80,1536]{1,0:T(8,128)(2,1)S(1)}, bf16[80,1536]{1,0:T(8,128)(2,1)S(1)}, u32[]{:S(2)}, u32[]{:S(2)}) collective-permute-start(bf16[80,1536]{1,0:T(8,128)(2,1)S(1)} %add_convert_fusion.8), channel_id=1, source_target_pairs={{0,2},{1,3},{2,4},{3,5},{4,6},{5,7},{6,8},{7,9},{8,10},{9,11},{10,... | collective-permute-start | bytes 737288 | tf_op jit(solution)/shard_map/ppermute | solution.py:33
  147.5 5.4 %collective-permute-start.34 = (bf16[80,1536]{1,0:T(8,128)(2,1)S(1)}, bf16[80,1536]{1,0:T(8,128)(2,1)S(1)}, u32[]{:S(2)}, u32[]{:S(2)}) collective-permute-start(bf16[80,1536]{1,0:T(8,128)(2,1)S(1)} %add_convert_fusion.1), channel_id=1, source_target_pairs={{0,1},{1,0},{2,3},{3,2},{4,5},{5,4},{6,7},{7,6},{8,9},{9,8},{10,11... | collective-permute-start | bytes 737288 | tf_op jit(solution)/shard_map/ppermute | solution.py:37
  152.9 0.7 copy-start.25
  (1 other events, 0.6 us)
Sparse Core Ops, SparseCore 0:
  10.4 52.4 all-gather.1
  143.0 36.4 reduce-scatter.1
